TPU v7x, 128 devices: a whole 4x4x4 slice. The times are simulated.
128 devices in a mesh: tile: 32 (over x, z, core), rep: 4 (over y).
Axes of the slice: x: 4, y: 4, z: 4, core: 2. Of those that a mesh axis runs over, the one named last changes fastest.
Arguments:
- source: bfloat16 [32768, 256], P('tile'), may hold values from -20 to 20
- target: bfloat16 [32768, 256], P(('rep', 'tile')), may hold values from -20 to 20
- row_logw: float32 [32768], P('tile'), may hold values from -4 to 4
- col_logw: float32 [32768], P(('rep', 'tile')), may hold values from -4 to 4
- support: int32 [32, 32], replicated, may hold values from 0 to 1, as said below
Outputs:
- row_dual: float32 [32768], P('tile')
- col_dual: float32 [32768], P(('rep', 'tile'))
Inputs may be any that keep to these rules, and one draw needn't show every extreme that they name: `support`: entries are 0 or 1; every row of blocks and every column of blocks holds at least one 1.
All inputs are finite; a program needn't handle non-finite values.
Results may differ from a plain program's by a relative error of at most 0.0004.
Values may be sent and summed in bfloat16 or wider, within the bound.
A program may use at most 128 MiB of HBM per device.

v0:
```python
import jax
import jax.numpy as jnp
from jax import lax
from jax.sharding import PartitionSpec as P

ITERS = 2


EPS = 0.1
NEG = -1e30


def merged(part, axis, combine):
    gathered = jax.tree.map(lambda a: lax.all_gather(a, axis), part)

    def take(source):
        return jax.tree.map(lambda a: lax.dynamic_index_in_dim(a, source, 0, False), gathered)

    return lax.fori_loop(
        1, lax.axis_size(axis), lambda source, state: combine(state, take(source)), take(0)
    )


def merge_pairs(first, second):
    peak = jnp.maximum(first[0], second[0])
    return (peak, first[1] * jnp.exp(first[0] - peak) + second[1] * jnp.exp(second[0] - peak))


def cost_piece(source_rows, row_sq, shard_rows):
    product = lax.dot_general(
        source_rows, shard_rows, (((1,), (1,)), ((), ())), preferred_element_type=jnp.float32
    )
    col_sq = jnp.sum(jnp.square(shard_rows.astype(jnp.float32)), axis=1)
    return (row_sq[:, None] + col_sq[None, :] - 2.0 * product) / source_rows.shape[1]


def row_partial(source_rows, row_sq, shard_rows, col_pot, kept):
    score = jnp.where(
        kept[None, :], (col_pot[None, :] - cost_piece(source_rows, row_sq, shard_rows)) / EPS, NEG
    )
    peak = jnp.max(score, axis=1)
    total = jnp.sum(jnp.where(kept[None, :], jnp.exp(score - peak[:, None]), 0.0), axis=1)
    return (peak, total)


def col_partial(source_rows, row_sq, shard_rows, dual, kept):
    score = jnp.where(
        kept[None, :], (dual[:, None] - cost_piece(source_rows, row_sq, shard_rows)) / EPS, NEG
    )
    peak = jnp.max(score, axis=0)
    total = jnp.sum(jnp.where(kept[None, :], jnp.exp(score - peak[None, :]), 0.0), axis=0)
    return (peak, total)


def flag_at(flags, block):
    return jnp.any(flags & (jnp.arange(flags.shape[0], dtype=jnp.int32) == block))


def block_turns(piece, offset, block_rows, shard, visit, carry):
    count = piece.shape[0]
    span = min(count, block_rows)
    turns = min(count // shard, (block_rows - shard + count - 1) // block_rows + 1)
    last = (offset + count - 1) // block_rows

    def one_turn(step, state):
        begin = jnp.clip(step * block_rows, 0, count - span)
        columns = lax.dynamic_slice_in_dim(piece, begin, span)
        spots = begin + jnp.arange(span, dtype=jnp.int32)
        kept = spots // block_rows == step
        return visit(state, step, step <= last, columns, begin, kept)

    return lax.fori_loop(0, turns, one_turn, carry)


def listed_step(visit, block_rows, shard):

    def fold_piece(carry, piece, offset):
        return block_turns(piece, offset, block_rows, shard, visit, carry)

    return fold_piece


def row_tenant(tenant, pair, block, inside, columns, col_pot, kept):
    source_rows, squares, flags = tenant

    def row_compute(current):
        return merge_pairs(current, row_partial(source_rows, squares, columns, col_pot, kept))

    def row_keep_same(current):
        return current

    return lax.cond(inside & flag_at(flags, block), row_compute, row_keep_same, pair)


def row_visitor(tenants, potential):

    def visit(state, block, inside, columns, start, kept):
        col_pot = lax.dynamic_slice_in_dim(potential, start, columns.shape[0])
        updated = []
        for tenant, pair in zip(tenants, state):
            updated.append(row_tenant(tenant, pair, block, inside, columns, col_pot, kept))
        return tuple(updated)

    return visit


def col_tenant(tenant, fresh, block, inside, columns, kept):
    source_rows, squares, flags, dual = tenant

    def col_compute(current):
        return merge_pairs(current, col_partial(source_rows, squares, columns, dual, kept))

    def col_keep_same(current):
        return current

    return lax.cond(inside & flag_at(flags, block), col_compute, col_keep_same, fresh)


def col_visitor(tenants):

    def visit(state, block, inside, columns, start, kept):
        span = columns.shape[0]
        fresh = (jnp.full((span,), NEG, jnp.float32), jnp.zeros((span,), jnp.float32))
        for tenant in tenants:
            fresh = col_tenant(tenant, fresh, block, inside, columns, kept)
        old_peak = lax.dynamic_slice_in_dim(state[0], start, span)
        old_total = lax.dynamic_slice_in_dim(state[1], start, span)
        new_peak = lax.dynamic_update_slice_in_dim(
            state[0], jnp.where(kept, fresh[0], old_peak), start, 0
        )
        new_total = lax.dynamic_update_slice_in_dim(
            state[1], jnp.where(kept, fresh[1], old_total), start, 0
        )
        return (new_peak, new_total)

    return visit


def per_device(source, target, row_logw, col_logw, support):
    rep_count = lax.axis_size("rep")
    block_rows = source.shape[0]
    shard = target.shape[0]
    group = support.shape[1] // rep_count
    width = group * block_rows
    row_index = lax.axis_index("tile")
    rep_index = lax.axis_index("rep")
    owned = col_logw.shape[0]
    blocks_live = lax.dynamic_slice(support, (row_index, rep_index * group), (1, group))[0]
    row_sq = jnp.sum(jnp.square(source.astype(jnp.float32)), axis=1)
    tenants = [(source, row_sq, blocks_live > 0)]
    potential = jnp.zeros((width,), jnp.float32)
    row_dual = None
    col_owned = None
    for iteration in range(ITERS):
        row_start = (
            jnp.full((block_rows,), NEG, jnp.float32),
            jnp.zeros((block_rows,), jnp.float32),
        )
        row_step = listed_step(row_visitor(tenants, potential), block_rows, shard)
        row_init = tuple((row_start for tenant in tenants))
        partial_value = row_step(
            row_init, lax.all_gather(target, "tile", axis=0, tiled=True), jnp.int32(0)
        )
        own_part = partial_value[0]
        row_peak, row_total = merged(own_part, "rep", merge_pairs)
        row_dual = EPS * (row_logw - (row_peak + jnp.log(row_total)))
        col_start = (jnp.full((width,), NEG, jnp.float32), jnp.zeros((width,), jnp.float32))
        col_tenants = [tenants[0] + (row_dual,)]
        col_step = listed_step(col_visitor(col_tenants), block_rows, shard)
        col_peaks, col_totals = col_step(
            col_start, lax.all_gather(target, "tile", axis=0, tiled=True), jnp.int32(0)
        )
        global_peak = lax.pmax(col_peaks.astype(jnp.bfloat16), "tile").astype(col_peaks.dtype)
        shifted = col_totals * jnp.exp(col_peaks - global_peak)
        owned_total = lax.psum_scatter(
            shifted.astype(jnp.bfloat16), "tile", scatter_dimension=0, tiled=True
        ).astype(jnp.float32)
        owned_peak = lax.dynamic_slice_in_dim(global_peak, row_index * owned, owned)
        col_owned = EPS * (col_logw - (owned_peak + jnp.log(owned_total)))
        if iteration + 1 < ITERS:
            potential = lax.all_gather(col_owned, "tile", axis=0, tiled=True)
    return (row_dual, col_owned)


def solution(mesh):
    placed = (P("tile", None), P(("rep", "tile"), None), P("tile"), P(("rep", "tile")), P())
    return jax.shard_map(
        per_device,
        mesh=mesh,
        in_specs=placed,
        out_specs=(P("tile"), P(("rep", "tile"))),
        check_vma=False,
    )
```

profile of v0, /device:TPU:1, one launch (start us, length us, event | category | flops | bytes accessed | tf_op | source)
XLA Modules:
  0.0 854.1 jit_solution(5606178424058438489)
XLA Ops:
  11.7 48.6 %all-gather.7.cloned.1.call-done = bf16[8192,256]{1,0:T(8,128)(2,1)} async-done(((bf16[256,256]{1,0:T(8,128)(2,1)}), bf16[8192,256]{1,0:T(8,128)(2,1)}) %all-gather.7.cloned.1.call-update) | async-done | bytes 4194320 | tf_op jit(solution)/shard_map/all_gather | solution.py:162
  60.3 38.3 %while.102 = (s32[]{:T(128)}, f32[1024]{0:T(1024)S(1)}, f32[1024]{0:T(1024)S(1)}, pred[8]{0:T(512)(128)(4,1)S(1)}, f32[1024]{0:T(1024)S(1)}, /*index=5*/bf16[819...) while((s32[]{:T(128)}, f32[1024]{0:T(1024)S(1)}, ...), condition=%wide.region_8.9_spmd, body=%wide.region_1.8_spmd.sunk | while | flops 556552192 | bytes 10030911 | solution.py:72
  63.1 6.4 conditional.8
  63.2 1.3 multiply_reduce_fusion.2
  64.5 2.9 fusion.28
  67.4 2.1 select_reduce_fusion.2
  70.9 6.3 conditional.8
  70.9 1.3 multiply_reduce_fusion.2
  72.3 2.9 fusion.28
  75.2 2.1 select_reduce_fusion.2
  81.6 6.4 conditional.8
  82.9 2.9 fusion.28
  85.8 2.1 select_reduce_fusion.2
  89.3 6.4 conditional.8
  90.7 2.9 fusion.28
  93.6 2.1 select_reduce_fusion.2
  98.6 9.4 %all-gather = f32[4096]{0:T(1024)S(1)} all-gather(f32[1024]{0:T(1024)S(1)} %get-tuple-element.1636), channel_id=2, replica_groups=mesh['tile'=32,'rep'=4] {'rep'}, dimensions={0}, use_global_device_ids=true | all-gather | bytes 20480 | tf_op jit(solution)/shard_map/all_gather | solution.py:14
  108.0 9.0 %all-gather.1 = f32[4096]{0:T(1024)S(1)} all-gather(f32[1024]{0:T(1024)S(1)} %get-tuple-element.1637), channel_id=3, replica_groups=mesh['tile'=32,'rep'=4] {'rep'}, dimensions={0}, use_global_device_ids=true | all-gather | bytes 20480 | tf_op jit(solution)/shard_map/all_gather | solution.py:14
  117.3 37.8 %while.104 = (s32[]{:T(128)}, f32[8192]{0:T(1024)S(1)}, f32[8192]{0:T(1024)S(1)}, pred[8]{0:T(512)(128)(4,1)S(1)}, f32[1024]{0:T(1024)S(1)}, /*index=5*/f32[1024...) while((s32[]{:T(128)}, f32[8192]{0:T(1024)S(1)}, ...), condition=%wide.region_18.19_spmd, body=%wide.region_11.18_spmd.sunk | while | flops 556571648 | bytes 10048779 | solution.py:72
  120.0 6.1 conditional.9
  121.4 2.8 fusion.4
  124.1 2.0 select_reduce_fusion
  127.6 6.1 conditional.9
  128.9 2.8 fusion.4
  131.7 2.0 select_reduce_fusion
  138.2 6.1 conditional.9
  139.5 2.8 fusion.4
  142.3 2.0 select_reduce_fusion
  145.8 6.1 conditional.9
  147.1 2.8 fusion.4
  149.9 2.0 select_reduce_fusion
  155.1 161.1 %pmax.14 = bf16[8192]{0:T(1024)(128)(2,1)S(1)} all-reduce(bf16[8192]{0:T(1024)(128)(2,1)S(1)} %convert_element_type.91), channel_id=1, replica_groups=mesh['tile'=32,'rep'=4] {'tile'}, use_global_device_ids=true, to_apply=%region_19.20 | all-reduce | flops 8192 | bytes 32768 | tf_op jit(solution)/shard_map/pmax | solution.py:173
  316.2 123.8 %all-reduce = bf16[8192]{0:T(1024)(128)(2,1)S(1)} all-reduce(bf16[8192]{0:T(1024)(128)(2,1)S(1)} %multiply_convert_fusion.1), channel_id=6, replica_groups=mesh['tile'=32,'rep'=4] {'tile'}, use_global_device_ids=true, to_apply=%region_20.21.clone | all-reduce | flops 8192 | bytes 32768
  440.1 25.8 %all-gather.4 = f32[32,1,256]{2,1,0:T(1,128)S(1)} all-gather(f32[1,1,256]{2,1,0:T(1,128)S(1)} %bitcast.82), channel_id=1, replica_groups=mesh['tile'=32,'rep'=4] {'tile'}, dimensions={0}, use_global_device_ids=true | all-gather | bytes 33792 | tf_op jit(solution)/shard_map/all_gather | solution.py:181
  465.9 38.5 %while.105 = (s32[]{:T(128)}, f32[1024]{0:T(1024)S(1)}, f32[1024]{0:T(1024)S(1)}, pred[8]{0:T(512)(128)(4,1)S(1)}, f32[8192]{0:T(1024)S(1)}, /*index=5*/f32[1024...) while((s32[]{:T(128)}, f32[1024]{0:T(1024)S(1)}, ...), condition=%wide.region_28.29_spmd, body=%wide.region_21.28_spmd.sunk | while | flops 556552192 | bytes 10047315 | solution.py:72
  468.8 6.4 conditional.10
  470.2 2.9 fusion.39
  473.1 2.0 select_reduce_fusion.3
  476.6 6.4 conditional.10
  478.0 2.9 fusion.39
  481.0 2.0 select_reduce_fusion.3
  487.3 6.4 conditional.10
  488.7 2.9 fusion.39
  491.7 2.0 select_reduce_fusion.3
  495.1 6.4 conditional.10
  496.6 2.9 fusion.39
  499.5 2.0 select_reduce_fusion.3
  504.4 9.0 %all-gather.2 = f32[4096]{0:T(1024)S(1)} all-gather(f32[1024]{0:T(1024)S(1)} %get-tuple-element.1642), channel_id=4, replica_groups=mesh['tile'=32,'rep'=4] {'rep'}, dimensions={0}, use_global_device_ids=true | all-gather | bytes 20480 | tf_op jit(solution)/shard_map/all_gather | solution.py:14
  513.5 9.0 %all-gather.3 = f32[4096]{0:T(1024)S(1)} all-gather(f32[1024]{0:T(1024)S(1)} %get-tuple-element.1643), channel_id=5, replica_groups=mesh['tile'=32,'rep'=4] {'rep'}, dimensions={0}, use_global_device_ids=true | all-gather | bytes 20480 | tf_op jit(solution)/shard_map/all_gather | solution.py:14
  522.8 38.4 %while.107 = (s32[]{:T(128)}, f32[8192]{0:T(1024)S(1)}, f32[8192]{0:T(1024)S(1)}, pred[8]{0:T(512)(128)(4,1)S(1)}, f32[1024]{0:T(1024)S(1)}, /*index=5*/f32[1024...) while((s32[]{:T(128)}, f32[8192]{0:T(1024)S(1)}, ...), condition=%wide.region_38.39_spmd, body=%wide.region_31.38_spmd.sunk | while | flops 556571648 | bytes 10048779 | solution.py:72
  525.7 6.1 conditional.11
  527.0 2.8 fusion.16
  529.8 2.0 select_reduce_fusion.1
  533.3 6.1 conditional.11
  534.6 2.8 fusion.16
  537.4 2.0 select_reduce_fusion.1
  544.1 6.1 conditional.11
  545.4 2.8 fusion.16
  548.2 2.0 select_reduce_fusion.1
  551.7 6.1 conditional.11
  553.1 2.8 fusion.16
  555.8 2.0 select_reduce_fusion.1
  561.2 161.5 %pmax.15 = bf16[8192]{0:T(1024)(128)(2,1)S(1)} all-reduce(bf16[8192]{0:T(1024)(128)(2,1)S(1)} %convert_element_type.95), channel_id=1, replica_groups=mesh['tile'=32,'rep'=4] {'tile'}, use_global_device_ids=true, to_apply=%region_39.40 | all-reduce | flops 8192 | bytes 32768 | tf_op jit(solution)/shard_map/pmax | solution.py:173
  722.7 123.8 %all-reduce.1 = bf16[8192]{0:T(1024)(128)(2,1)S(1)} all-reduce(bf16[8192]{0:T(1024)(128)(2,1)S(1)} %multiply_convert_fusion), channel_id=7, replica_groups=mesh['tile'=32,'rep'=4] {'tile'}, use_global_device_ids=true, to_apply=%region_40.41.clone | all-reduce | flops 8192 | bytes 32768
  (223 shorter events, 53.1 us)
Async XLA Ops:
  7.2 53.1 %all-gather.7.cloned.1.call-start = ((), (), s32[]{:S(2)}) async-start(), calls=%async_computation | async-start | bytes 4325376 | tf_op jit(solution)/shard_map/all_gather | solution.py:162
  60.3 56.9 %copy-start.1 = (f32[1024]{0:T(1024)S(1)}, f32[1024]{0:T(1024)}, u32[]{:S(2)}) copy-start(f32[1024]{0:T(1024)} %param.27) | copy-start | bytes 12292
  117.3 322.8 %copy-start.2 = (f32[256]{0:T(256)S(1)}, f32[256]{0:T(256)}, u32[]{:S(2)}) copy-start(f32[256]{0:T(256)} %param.28) | copy-start | bytes 3076
  561.2 286.0 %copy-start = (f32[1024]{0:T(1024)}, f32[1024]{0:T(1024)S(1)}, u32[]{:S(2)}) copy-start(f32[1024]{0:T(1024)S(1)} %get-tuple-element.2338) | copy-start | bytes 12292
Sparse Core Ops, SparseCore 0:
  10.3 49.9 all-gather.6
where the time goes:
time: 861 us; the launch traced here: 854 us
  blocking collectives  633 us (74%)
  other arithmetic  84.4 us (10%)
  waiting for transfers between devices  49.2 us (6%)
  matrix products  45.6 us (5%)
  loops' own time  25.6 us (3%)
  between operations  14.7 us (2%)
    pmax x2, blocking collectives, per_device(): lax.pmax(col_peaks.astype(jnp.bfloat16), 'tile').astype(col_peaks.dtype)  323 us
    unnamed x2, blocking collectives  248 us
    all_gather x1, waiting for transfers between devices, per_device(): lax.all_gather(target, 'tile', axis=0, tiled=True)  48.6 us
    dot_general x16, matrix products, cost_piece(): lax.dot_general(source_rows, shard_rows, (((1,), (1,)), ((), ())), prefer...  45.6 us
    all_gather x4, blocking collectives, merged(): gathered = jax.tree.map(lambda a: lax.all_gather(a, axis), part)  36.5 us
    all_gather x1, blocking collectives, per_device(): potential = lax.all_gather(col_owned, 'tile', axis=0, tiled=True)  25.8 us
    another operation x4, loops' own time, block_turns(): return lax.fori_loop(0, turns, one_turn, carry)  24.4 us
    reduce_or x36, other arithmetic, flag_at(): jnp.any(flags & (jnp.arange(flags.shape[0], dtype=jnp.int32) == block))  24.2 us
  transfers between devices with their start and end apart: 1, of which 1 were waited for; matrix products, arithmetic and copies ran while one was open for 0% of the time, Pallas kernels for 0%

commit v1 on v0

v1 whole, which is shorter than its diff:
```python
import functools
import math

import jax
import jax.numpy as jnp
from jax import lax
from jax.experimental import pallas as pl
from jax.experimental.pallas import tpu as pltpu
from jax.sharding import PartitionSpec as P

MESH = pl.DeviceIdType.MESH
ITERS = 2
EPS = 0.1
NEG = -1e30
LOG2E = 1.0 / math.log(2.0)
LN2 = math.log(2.0)
NX = 4
TILES = 2 * NX * NX
REPS = 4
LANES = 128


def kernel(
    source_hbm,
    target_hbm,
    row_logw,
    col_logw,
    support,
    row_out,
    col_out,
    src,
    tgt,
    prod,
    m_run,
    s_run,
    b_col,
    a_all,
    a_wide,
    row_part,
    col_part,
    col_in,
    local_sem,
    gather_send,
    gather_recv,
    a_send,
    a_recv,
    row_send,
    row_recv,
    col_send,
    col_recv,
):
    rows = src.shape[0]
    shard = tgt.shape[1]
    depth = src.shape[1]
    blocks = TILES * shard // rows
    per_block = TILES // blocks
    chunks = rows // LANES
    me = lax.axis_index("tile")
    rep = lax.axis_index("rep")
    core = me % 2
    x = me // (2 * NX)
    z = (me // 2) % NX
    first = x * (1 - core) + z * core
    second = z * (1 - core) + x * core
    score_scale = 2.0 * LOG2E / (depth * EPS)
    square_scale = LOG2E / (depth * EPS)
    dual_scale = EPS * LN2

    def tile_of(core_id, da, db):
        a = (first + da + NX) % NX
        b = (second + db + NX) % NX
        return ((a * NX + b) * (1 - core_id) + (b * NX + a) * core_id) * 2 + core_id

    def mine(da, db):
        return tile_of(core, da, db)

    partner = me + 1 - 2 * core

    def partners(da, db):
        a = (second + da + NX) % NX
        b = (first + db + NX) % NX
        other = 1 - core
        return ((a * NX + b) * (1 - other) + (b * NX + a) * other) * 2 + other

    barrier = pltpu.get_barrier_semaphore()

    def greet(step, carry):
        to = (me + step) % TILES
        pl.semaphore_signal(barrier, inc=1, device_id={"tile": to}, device_id_type=MESH)
        return carry

    load_src = pltpu.make_async_copy(source_hbm, src, local_sem.at[0])
    load_src.start()
    load_tgt = pltpu.make_async_copy(target_hbm, tgt.at[me], local_sem.at[1])
    load_tgt.start()
    lax.fori_loop(1, TILES, greet, 0)
    for step in range(1, REPS):
        to = (rep + step) % REPS
        pl.semaphore_signal(barrier, inc=1, device_id={"rep": to}, device_id_type=MESH)
    pl.semaphore_wait(barrier, TILES - 1 + REPS - 1)

    half = shard // 2

    def send_shard(k, to, part=None, source=None):
        if part is None:
            view, sem = tgt.at[k], gather_recv.at[0, k]
        else:
            view, sem = tgt.at[k, pl.ds(part * half, half)], gather_recv.at[part, k]
        pltpu.make_async_remote_copy(
            src_ref=view if source is None else source,
            dst_ref=view,
            send_sem=gather_send.at[0],
            recv_sem=sem,
            device_id={"tile": to},
            device_id_type=MESH,
        ).start()

    def wait_shard(k, parts):
        if parts == 1:
            pltpu.make_async_copy(tgt.at[k], tgt.at[k], gather_recv.at[0, k]).wait()
        else:
            for part in range(2):
                view = tgt.at[k, pl.ds(part * half, half)]
                pltpu.make_async_copy(view, view, gather_recv.at[part, k]).wait()

    send_shard(me, mine(1, 0), source=target_hbm)
    send_shard(me, mine(-1, 0), source=target_hbm)
    send_shard(me, mine(0, 1), source=target_hbm)
    send_shard(me, mine(0, -1), source=target_hbm)
    send_shard(me, partner, source=target_hbm)

    def send_potential(iteration):
        def one(step, carry):
            to = (me + step) % TILES
            pltpu.make_async_remote_copy(
                src_ref=a_all.at[iteration, me],
                dst_ref=a_all.at[iteration, me],
                send_sem=a_send.at[iteration],
                recv_sem=a_recv.at[iteration],
                device_id={"tile": to},
                device_id_type=MESH,
            ).start()
            return carry

        lax.fori_loop(1, TILES, one, 0)

    def wait_potential(iteration):
        view = a_all.at[iteration, pl.ds(0, TILES - 1)]
        pltpu.make_async_copy(view, view, a_recv.at[iteration]).wait()

    def bias_of(k):
        live = support[me, rep * blocks + k // per_block]
        return (1.0 - live.astype(jnp.float32)) * NEG

    load_tgt.wait()
    own = tgt[me].astype(jnp.float32)
    own_sq = jnp.sum((own * own).T, axis=0, keepdims=True)
    a_all[0, me] = -square_scale * own_sq
    send_potential(0)

    m_run[...] = jnp.full(m_run.shape, NEG, jnp.float32)
    s_run[...] = jnp.zeros(s_run.shape, jnp.float32)
    load_src.wait()

    row_block = min(512, rows)

    def first_rows(k):
        a = a_all[0, k] + bias_of(k)
        cells = tgt[k]

        def some(step, carry):
            at = pl.ds(pl.multiple_of(step * row_block, row_block), row_block)
            p = score_scale * lax.dot_general(
                src[at, :], cells, (((1,), (1,)), ((), ())), preferred_element_type=jnp.float32
            )
            prod[k, at, :] = p
            old = m_run[at, :]
            t = [
                p[:, i * LANES : (i + 1) * LANES] + a[:, i * LANES : (i + 1) * LANES]
                for i in range(shard // LANES)
            ]
            new = functools.reduce(jnp.maximum, t, old)
            m_run[at, :] = new
            s_run[at, :] = s_run[at, :] * jnp.exp2(old - new) + sum(jnp.exp2(v - new) for v in t)
            return carry

        lax.fori_loop(0, rows // row_block, some, 0)

    k = mine(-1, 0)
    wait_shard(k, 1)
    for to in (mine(0, 1), mine(0, -1)):
        send_shard(k, to)
    send_shard(k, mine(1, 0), part=0)
    send_shard(k, partner)
    k = mine(1, 0)
    wait_shard(k, 1)
    for to in (mine(0, 1), mine(0, -1)):
        send_shard(k, to)
    send_shard(k, mine(-1, 0), part=1)
    send_shard(k, partner)
    wait_potential(0)
    first_rows(me)

    def pass_along_second(da):
        k = mine(da, -1)
        wait_shard(k, 1)
        send_shard(k, mine(0, 1), part=0)
        send_shard(k, partner)
        k = mine(da, 1)
        wait_shard(k, 1)
        send_shard(k, mine(0, -1), part=1)
        send_shard(k, partner)

    k = mine(2, 0)
    wait_shard(k, 2)
    for to in (mine(0, 1), mine(0, -1)):
        send_shard(k, to)
    send_shard(k, partner)
    pass_along_second(0)
    k = partner
    wait_shard(k, 1)
    first_rows(k)
    first_rows(mine(-1, 0))
    first_rows(mine(1, 0))
    pass_along_second(-1)
    first_rows(mine(2, 0))
    first_rows(mine(0, -1))
    first_rows(mine(0, 1))
    pass_along_second(1)
    for da, db in ((-1, 0), (1, 0), (2, 0), (0, -1), (0, 1)):
        k = partners(da, db)
        wait_shard(k, 1)
        first_rows(k)
    pass_along_second(2)
    for da in (-1, 1, 2):
        first_rows(mine(da, -1))
        first_rows(mine(da, 1))
    for da in (0, -1, 1, 2):
        k = mine(da, 2)
        wait_shard(k, 2)
        send_shard(k, partner)
    for da in (-1, 1, 2):
        for db in (-1, 1):
            k = partners(da, db)
            wait_shard(k, 1)
            first_rows(k)
    for da in (0, -1, 1, 2):
        first_rows(mine(da, 2))
    for da in (0, -1, 1, 2):
        k = partners(da, 2)
        wait_shard(k, 1)
        first_rows(k)

    def send_view(parts):
        return tgt.at[pl.ds(0, parts)]

    def finish_rows(iteration):
        def fold(q, carry):
            at = pl.ds(pl.multiple_of(q * LANES, LANES), LANES)
            m = m_run[at, :].T
            s = s_run[at, :].T
            peak = jnp.max(m, axis=0, keepdims=True)
            total = jnp.sum(s * jnp.exp2(m - peak), axis=0, keepdims=True)
            row_part[iteration, rep, pl.ds(q, 1), :] = peak + jnp.log2(total)
            return carry

        lax.fori_loop(0, chunks, fold, 0)
        for step in range(1, REPS):
            to = (rep + step) % REPS
            pltpu.make_async_remote_copy(
                src_ref=row_part.at[iteration, rep],
                dst_ref=row_part.at[iteration, rep],
                send_sem=row_send.at[iteration],
                recv_sem=row_recv.at[iteration],
                device_id={"rep": to},
                device_id_type=MESH,
            ).start()
        view = row_part.at[iteration, pl.ds(0, REPS - 1)]
        pltpu.make_async_copy(view, view, row_recv.at[iteration]).wait()
        parts = [row_part[iteration, i] for i in range(REPS)]
        peak = functools.reduce(jnp.maximum, parts)
        total = sum(jnp.exp2(v - peak) for v in parts)
        b = LOG2E * row_logw[...] - (peak + jnp.log2(total))
        for q in range(chunks):
            b_col[q * LANES : (q + 1) * LANES, :] = jnp.broadcast_to(
                b[q : q + 1, :], (LANES, LANES)
            ).T
        return b

    groups = LANES // 8

    def columns_of(k, iteration):
        bias = bias_of(k)
        for i in range(shard // LANES):
            lanes = slice(i * LANES, (i + 1) * LANES)
            peak = jnp.full((8, LANES), NEG, jnp.float32)
            total = jnp.zeros((8, LANES), jnp.float32)
            for q in range(chunks):
                at = slice(q * LANES, (q + 1) * LANES)
                t = (prod[k, at, lanes] + b_col[at, :]).reshape(groups, 8, LANES)
                new = jnp.maximum(peak, jnp.max(t, axis=0))
                total = total * jnp.exp2(peak - new) + jnp.sum(jnp.exp2(t - new[None]), axis=0)
                peak = new
            top = jnp.max(peak, axis=0, keepdims=True)
            total = jnp.sum(total * jnp.exp2(peak - top), axis=0, keepdims=True)
            col_part[iteration, k, :, lanes] = top + jnp.log2(total) + bias

    def column_pass(iteration):
        def one(step, carry):
            k = (me + step) % TILES
            columns_of(k, iteration)
            pltpu.make_async_remote_copy(
                src_ref=col_part.at[iteration, k],
                dst_ref=col_in.at[iteration, step - 1],
                send_sem=col_send.at[iteration],
                recv_sem=col_recv.at[iteration],
                device_id={"tile": k},
                device_id_type=MESH,
            ).start()
            return carry

        lax.fori_loop(1, TILES, one, 0)
        columns_of(me, iteration)
        col_in[iteration, TILES - 1] = col_part[iteration, me]
        view = col_in.at[iteration, pl.ds(0, TILES - 1)]
        pltpu.make_async_copy(view, view, col_recv.at[iteration]).wait()
        parts = col_in[iteration]
        peak = jnp.max(parts, axis=0)
        total = jnp.sum(jnp.exp2(parts - peak[None]), axis=0)
        return LOG2E * col_logw[...] - (peak + jnp.log2(total))

    step_rows = 16
    wide = 8

    def row_pass(iteration):
        def spread(k, carry):
            a = a_all[iteration, k] + bias_of(k)
            a_wide[k] = jnp.broadcast_to(a, (8, shard))
            return carry

        lax.fori_loop(0, TILES, spread, 0)

        def some(step, carry):
            at = pl.ds(pl.multiple_of(step * step_rows, step_rows), step_rows)
            peak = jnp.full((step_rows // 8, 8, LANES), NEG, jnp.float32)
            total = jnp.zeros((step_rows // 8, 8, LANES), jnp.float32)
            for k0 in range(0, TILES, wide):
                t = []
                for k in range(k0, k0 + wide):
                    p = prod[k, at, :].reshape(step_rows // 8, 8, shard) + a_wide[k][None]
                    t.extend(p[:, :, i * LANES : (i + 1) * LANES] for i in range(shard // LANES))
                new = functools.reduce(jnp.maximum, t, peak)
                total = total * jnp.exp2(peak - new) + sum(jnp.exp2(v - new) for v in t)
                peak = new
            m_run[at, :] = peak.reshape(step_rows, LANES)
            s_run[at, :] = total.reshape(step_rows, LANES)
            return carry

        lax.fori_loop(0, rows // step_rows, some, 0)

    b = finish_rows(0)
    a = column_pass(0)
    for iteration in range(1, ITERS):
        a_all[iteration, me] = a
        send_potential(iteration)
        wait_potential(iteration)
        row_pass(iteration)
        b = finish_rows(iteration)
        a = column_pass(iteration)

    for q in range(chunks):
        cells = src[q * LANES : (q + 1) * LANES, :].astype(jnp.float32)
        sq = cells * cells
        sq = sum(sq[:, i * LANES : (i + 1) * LANES] for i in range(depth // LANES))
        row_out[q : q + 1, :] = jnp.sum(sq.T, axis=0, keepdims=True) / depth
    row_out[...] = row_out[...] + dual_scale * b
    col_out[...] = own_sq / depth + dual_scale * a

    view = send_view(TILES - 1)
    pltpu.make_async_copy(view, view, gather_send.at[0]).wait()
    for iteration in range(ITERS):
        view = a_all.at[iteration, pl.ds(0, TILES - 1)]
        pltpu.make_async_copy(view, view, a_send.at[iteration]).wait()
        view = row_part.at[iteration, pl.ds(0, REPS - 1)]
        pltpu.make_async_copy(view, view, row_send.at[iteration]).wait()
        view = col_part.at[iteration, pl.ds(0, TILES - 1)]
        pltpu.make_async_copy(view, view, col_send.at[iteration]).wait()


def per_device(source, target, row_logw, col_logw, support):
    rows, depth = source.shape
    shard = target.shape[0]
    vmem = pl.BlockSpec(memory_space=pltpu.VMEM)
    row_dual, col_dual = pl.pallas_call(
        kernel,
        out_shape=(
            jax.ShapeDtypeStruct((rows // LANES, LANES), jnp.float32),
            jax.ShapeDtypeStruct((1, shard), jnp.float32),
        ),
        in_specs=[
            pl.BlockSpec(memory_space=pl.ANY),
            pl.BlockSpec(memory_space=pl.ANY),
            vmem,
            vmem,
            pl.BlockSpec(memory_space=pltpu.SMEM),
        ],
        out_specs=(vmem, vmem),
        scratch_shapes=[
            pltpu.VMEM((rows, depth), source.dtype),
            pltpu.VMEM((TILES, shard, depth), target.dtype),
            pltpu.VMEM((TILES, rows, shard), jnp.float32),
            pltpu.VMEM((rows, LANES), jnp.float32),
            pltpu.VMEM((rows, LANES), jnp.float32),
            pltpu.VMEM((rows, LANES), jnp.float32),
            pltpu.VMEM((ITERS, TILES, 1, shard), jnp.float32),
            pltpu.VMEM((TILES, 8, shard), jnp.float32),
            pltpu.VMEM((ITERS, REPS, rows // LANES, LANES), jnp.float32),
            pltpu.VMEM((ITERS, TILES, 1, shard), jnp.float32),
            pltpu.VMEM((ITERS, TILES, 1, shard), jnp.float32),
            pltpu.SemaphoreType.DMA((2,)),
            pltpu.SemaphoreType.DMA((1,)),
            pltpu.SemaphoreType.DMA((2, TILES)),
            pltpu.SemaphoreType.DMA((ITERS,)),
            pltpu.SemaphoreType.DMA((ITERS,)),
            pltpu.SemaphoreType.DMA((ITERS,)),
            pltpu.SemaphoreType.DMA((ITERS,)),
            pltpu.SemaphoreType.DMA((ITERS,)),
            pltpu.SemaphoreType.DMA((ITERS,)),
        ],
        compiler_params=pltpu.CompilerParams(
            collective_id=0, has_side_effects=True, vmem_limit_bytes=52 * 1024 * 1024
        ),
        name="sinkhorn",
    )(
        source,
        target,
        row_logw.reshape(rows // LANES, LANES),
        col_logw.reshape(1, shard),
        support,
    )
    return row_dual.reshape(rows), col_dual.reshape(shard)


def solution(mesh):
    placed = (P("tile", None), P(("rep", "tile"), None), P("tile"), P(("rep", "tile")), P())
    return jax.shard_map(
        per_device,
        mesh=mesh,
        in_specs=placed,
        out_specs=(P("tile"), P(("rep", "tile"))),
        check_vma=False,
    )
```

time: 861 us -> 90.6 us (0.11)
  blocking collectives: 633 us -> 0 us
  Pallas kernels: 0 us -> 84.5 us
  other arithmetic: 84.4 us -> 0 us
  waiting for transfers between devices: 49.2 us -> 0 us
  matrix products: 45.6 us -> 0 us
  loops' own time: 25.6 us -> 0 us
  between operations: 14.7 us -> 0.65 us
    pmax x2 -> x0, blocking collectives: 323 us -> none  [per_device(): lax.pmax(col_peaks.astype(jnp.bfloat16), 'tile').astype(col_peaks.dtype)]
    unnamed x2 -> x0, blocking collectives: 248 us -> none
    pallas_call x0 -> x1, Pallas kernels: none -> 84.5 us  [per_device(): pl.pallas_call(kernel, out_shape=(jax.ShapeDtypeStruct((rows // LANES, LA...]
    all_gather x5 -> x0, blocking collectives: 62.3 us -> none  [the longest x4 36.5 us: merged(): gathered = jax.tree.map(lambda a: lax.all_gather(a, axis), part)]
    reduce_sum x33 -> x0, other arithmetic: 54 us -> none  [the longest x16 20.7 us: cost_piece(): col_sq = jnp.sum(jnp.square(shard_rows.astype(jnp.float32)), axis=1)]
    all_gather x1 -> x0, waiting for transfers between devices: 48.6 us -> none  [per_device(): lax.all_gather(target, 'tile', axis=0, tiled=True)]
    dot_general x16 -> x0, matrix products: 45.6 us -> none  [cost_piece(): lax.dot_general(source_rows, shard_rows, (((1,), (1,)), ((), ())), prefer...]
    another operation x42 -> x0, loops' own time: 25.6 us -> none  [the longest x4 24.4 us: block_turns(): return lax.fori_loop(0, turns, one_turn, carry)]
  transfers between devices with their start and end apart: 1 -> 0, of which waited for: 1 -> 0; matrix products, arithmetic and copies ran while one was open for 0% -> 0% of each run, Pallas kernels for 0% -> 0%
where the time goes in v1:
time: 90.6 us; the launch traced here: 90.3 us
  Pallas kernels  84.5 us (93%)
  local copies, waits for them, and re-layouts  5.18 us (6%)
    pallas_call x1, Pallas kernels, per_device(): pl.pallas_call(kernel, out_shape=(jax.ShapeDtypeStruct((rows // LANES, LA...  84.5 us
    unnamed x12, local copies, waits for them, and re-layouts  5.18 us

profile of v1, /device:TPU:1, one launch (start us, length us, event | category | flops | bytes accessed | tf_op | source)
XLA Modules:
  0.0 90.3 jit_solution(3957885991713052379)
XLA Ops:
  0.6 0.0 copy-start.4
  0.6 0.7 copy-done.4
  1.3 0.0 copy-start
  1.3 1.0 %copy-done = bf16[1024,256]{1,0:T(8,128)(2,1)S(1)} copy-done((bf16[1024,256]{1,0:T(8,128)(2,1)S(1)}, bf16[1024,256]{1,0:T(8,128)(2,1)}, u32[]{:S(2)}) %copy-start) | copy-done | bytes 524312
  2.4 0.0 copy-start.1
  2.4 0.9 copy-done.1
  3.3 0.0 copy-start.2
  3.3 0.7 copy-done.2
  4.0 0.0 copy-start.3
  4.0 0.7 copy-done.3
  4.7 84.5 %sinkhorn.1 = (f32[8,128]{1,0:T(8,128)S(1)}, f32[1,256]{1,0:T(1,128)S(1)}) custom-call(bf16[1024,256]{1,0:T(8,128)(2,1)S(1)} %copy-done, bf16[256,256]{1,0:T(8,128)(2,1)S(1)} %copy-done.1, f32[8,128]{1,0:T(8,128)S(1)} %bitcast.4, f32[1,256]{1,0:T(1,128)S(1)} %bitcast.6, s32[32,32]{1,0:T(8,128)S(1)} %copy-done.2), custom_call_target="tpu_custom_call" | custom-call | tf_op jit(solution)/shard_map/sinkhorn/pallas_call | solution.py:394
  89.1 0.6 copy.9
  89.7 0.6 copy.10
Async XLA Ops:
  0.6 0.7 copy-start.4
  1.3 1.0 %copy-start = (bf16[1024,256]{1,0:T(8,128)(2,1)S(1)}, bf16[1024,256]{1,0:T(8,128)(2,1)}, u32[]{:S(2)}) copy-start(bf16[1024,256]{1,0:T(8,128)(2,1)} %source_hbm.1) | copy-start | bytes 1572868
  2.4 0.9 %copy-start.1 = (bf16[256,256]{1,0:T(8,128)(2,1)S(1)}, bf16[256,256]{1,0:T(8,128)(2,1)}, u32[]{:S(2)}) copy-start(bf16[256,256]{1,0:T(8,128)(2,1)} %target_hbm.1) | copy-start | bytes 393220
  3.3 0.7 copy-start.2
  4.0 0.7 copy-start.3

commit v2 on v1

v2 whole, which is shorter than its diff:
```python
import functools
import math

import jax
import jax.numpy as jnp
from jax import lax
from jax.experimental import pallas as pl
from jax.experimental.pallas import tpu as pltpu
from jax.sharding import PartitionSpec as P

MESH = pl.DeviceIdType.MESH
EPS = 0.1
NEG = -1e30
LOG2E = 1.0 / math.log(2.0)
LN2 = math.log(2.0)
NX = 4
TILES = 2 * NX * NX
REPS = 4
LANES = 128


def kernel(
    source_hbm,
    target_hbm,
    row_logw_hbm,
    col_logw_hbm,
    support_hbm,
    row_out,
    col_out,
    src,
    tgt,
    row_logw,
    col_logw,
    support,
    prod,
    stage_a,
    stage_b,
    m_run,
    s_run,
    b_col,
    a_all,
    a_wide,
    row_sq,
    row_part,
    col_part,
    col_in,
    local_sem,
    gather_send,
    gather_recv,
    a_send,
    a_recv,
    row_send,
    row_recv,
    col_send,
    col_recv,
):
    rows = src.shape[0]
    shard = tgt.shape[1]
    depth = src.shape[1]
    blocks = TILES * shard // rows
    per_block = TILES // blocks
    chunks = rows // LANES
    halves = shard // LANES
    me = lax.axis_index("tile")
    rep = lax.axis_index("rep")
    core = me % 2
    x = me // (2 * NX)
    z = (me // 2) % NX
    first = x * (1 - core) + z * core
    second = z * (1 - core) + x * core
    score_scale = 2.0 * LOG2E / (depth * EPS)
    square_scale = LOG2E / (depth * EPS)
    dual_scale = EPS * LN2

    def mine(da, db):
        a = (first + da) % NX
        b = (second + db) % NX
        return ((a * NX + b) * (1 - core) + (b * NX + a) * core) * 2 + core

    def theirs(da, db):
        a = (second + da) % NX
        b = (first + db) % NX
        return ((a * NX + b) * core + (b * NX + a) * (1 - core)) * 2 + 1 - core

    partner = me + 1 - 2 * core

    def far_first(n):
        m = NX - 1 - n
        return m + m // 2 - 2 * (m // 3)

    def peer(step):
        dx = far_first(step // 8)
        dz = far_first((step // 2) % 4)
        dc = 1 - step % 2
        return (((x + dx) % NX) * NX + (z + dz) % NX) * 2 + (core + dc) % 2

    loads = [
        pltpu.make_async_copy(target_hbm, tgt.at[me], local_sem.at[0]),
        pltpu.make_async_copy(source_hbm, src, local_sem.at[1]),
        pltpu.make_async_copy(support_hbm, support, local_sem.at[2]),
        pltpu.make_async_copy(row_logw_hbm, row_logw, local_sem.at[3]),
        pltpu.make_async_copy(col_logw_hbm, col_logw, local_sem.at[4]),
    ]
    for load in loads:
        load.start()

    barrier = pltpu.get_barrier_semaphore()

    def greet(step, carry):
        pl.semaphore_signal(
            barrier, inc=1, device_id={"tile": peer(step)}, device_id_type=MESH
        )
        return carry

    lax.fori_loop(0, TILES - 1, greet, 0)
    for step in range(1, REPS):
        to = (rep + step) % REPS
        pl.semaphore_signal(barrier, inc=1, device_id={"rep": to}, device_id_type=MESH)
    pl.semaphore_wait(barrier, TILES - 1 + REPS - 1)

    def send_shard(k, to, source=None):
        view = tgt.at[k]
        pltpu.make_async_remote_copy(
            src_ref=view if source is None else source,
            dst_ref=view,
            send_sem=gather_send.at[0],
            recv_sem=gather_recv.at[k],
            device_id={"tile": to},
            device_id_type=MESH,
        ).start()

    def wait_shard(k):
        pltpu.make_async_copy(tgt.at[k], tgt.at[k], gather_recv.at[k]).wait()

    for step in (1, 3, 2):
        send_shard(me, mine(step, 0), source=target_hbm)
    send_shard(me, partner, source=target_hbm)
    for step in (1, 3, 2):
        send_shard(me, mine(0, step), source=target_hbm)

    def send_potential(iteration):
        def one(step, carry):
            pltpu.make_async_remote_copy(
                src_ref=a_all.at[iteration, me],
                dst_ref=a_all.at[iteration, me],
                send_sem=a_send.at[iteration],
                recv_sem=a_recv.at[iteration],
                device_id={"tile": peer(step)},
                device_id_type=MESH,
            ).start()
            return carry

        lax.fori_loop(0, TILES - 1, one, 0)

    def wait_potential(iteration):
        view = a_all.at[iteration, pl.ds(0, TILES - 1)]
        pltpu.make_async_copy(view, view, a_recv.at[iteration]).wait()

    def bias_of(k):
        live = support[me, rep * blocks + k // per_block]
        return (1.0 - live.astype(jnp.float32)) * NEG

    loads[0].wait()
    own = tgt[me].astype(jnp.float32)
    own_sq = jnp.sum((own * own).T, axis=0, keepdims=True)
    a_all[0, me] = -square_scale * own_sq
    send_potential(0)
    for load in loads[1:]:
        load.wait()

    m_run[...] = jnp.full(m_run.shape, NEG, jnp.float32)
    s_run[...] = jnp.zeros(s_run.shape, jnp.float32)
    for q in range(chunks):
        cells = src[q * LANES : (q + 1) * LANES, :].astype(jnp.float32)
        sq = cells * cells
        sq = sum(sq[:, i * LANES : (i + 1) * LANES] for i in range(depth // LANES))
        row_sq[q : q + 1, :] = jnp.sum(sq.T, axis=0, keepdims=True)

    tall = 512

    def products(pair, stage):
        for i, k in enumerate(pair):
            cells = tgt[k]
            for r in range(0, rows, tall):
                stage[i, r : r + tall, :] = lax.dot_general(
                    src[r : r + tall, :],
                    cells,
                    (((1,), (1,)), ((), ())),
                    preferred_element_type=jnp.float32,
                )

    def update(pair, stage):
        terms = [a_all[0, k] + bias_of(k) for k in pair]
        step = 32
        for r in range(0, rows, step):
            at = slice(r, r + step)
            t = []
            for i, k in enumerate(pair):
                p = stage[i, at, :] * score_scale
                prod[k, at, :] = p
                t.extend(
                    p[:, h * LANES : (h + 1) * LANES] + terms[i][:, h * LANES : (h + 1) * LANES]
                    for h in range(halves)
                )
            old = m_run[at, :]
            new = functools.reduce(jnp.maximum, t, old)
            m_run[at, :] = new
            s_run[at, :] = s_run[at, :] * jnp.exp2(old - new) + sum(jnp.exp2(v - new) for v in t)

    def handle(entry):
        whose, da, db = entry
        if whose == "theirs":
            k = theirs(da, db)
            wait_shard(k)
            return k
        k = mine(da, db)
        if da == 0 and db == 0:
            return k
        wait_shard(k)
        if db == 0:
            for step in (1, 3, 2):
                send_shard(k, mine(0, step))
        send_shard(k, partner)
        return k

    near = [(1, 0), (3, 0), (0, 1), (0, 3), (2, 0), (0, 2)]
    later = [(a, b) for b in (1, 3, 2) for a in (1, 3, 2)]
    later.sort(key=lambda ab: (ab[0] == 2) + (ab[1] == 2))
    order = [("mine", 0, 0), ("theirs", 0, 0)]
    order += [("mine",) + ab for ab in near] + [("theirs",) + ab for ab in near]
    for i in range(0, len(later), 3):
        order += [("mine",) + ab for ab in later[i : i + 3]]
        order += [("theirs",) + ab for ab in later[i : i + 3]]

    stages = (stage_a, stage_b)
    before = None
    for n in range(0, TILES, 2):
        pair = [handle(order[n]), handle(order[n + 1])]
        products(pair, stages[(n // 2) % 2])
        if n == 0:
            wait_potential(0)
        else:
            update(before, stages[(n // 2 + 1) % 2])
        before = pair
    update(before, stages[(TILES // 2 + 1) % 2])

    def exchange_rows(iteration):
        for step in range(1, REPS):
            to = (rep + step) % REPS
            pltpu.make_async_remote_copy(
                src_ref=row_part.at[iteration, rep],
                dst_ref=row_part.at[iteration, rep],
                send_sem=row_send.at[iteration],
                recv_sem=row_recv.at[iteration],
                device_id={"rep": to},
                device_id_type=MESH,
            ).start()
        view = row_part.at[iteration, pl.ds(0, REPS - 1)]
        pltpu.make_async_copy(view, view, row_recv.at[iteration]).wait()
        return [row_part[iteration, i] for i in range(REPS)]

    def spread_rows(values):
        for q in range(chunks):
            b_col[q * LANES : (q + 1) * LANES, :] = jnp.broadcast_to(
                values[q : q + 1, :], (LANES, LANES)
            ).T

    for q in range(chunks):
        at = slice(q * LANES, (q + 1) * LANES)
        m = m_run[at, :].T
        s = s_run[at, :].T
        peak = jnp.max(m, axis=0, keepdims=True)
        total = jnp.sum(s * jnp.exp2(m - peak), axis=0, keepdims=True)
        row_part[0, rep, q : q + 1, :] = peak + jnp.log2(total)
    parts = exchange_rows(0)
    peak = functools.reduce(jnp.maximum, parts)
    total = sum(jnp.exp2(v - peak) for v in parts)
    b = LOG2E * row_logw[...] - (peak + jnp.log2(total))
    spread_rows(b)

    groups = LANES // 8

    def log_columns(k):
        bias = bias_of(k)
        for i in range(halves):
            lanes = slice(i * LANES, (i + 1) * LANES)
            peak = jnp.full((8, LANES), NEG, jnp.float32)
            total = jnp.zeros((8, LANES), jnp.float32)
            for q in range(chunks):
                at = slice(q * LANES, (q + 1) * LANES)
                t = prod[k, at, lanes] + b_col[at, :]
                prod[k, at, lanes] = t
                t = t.reshape(groups, 8, LANES)
                new = jnp.maximum(peak, jnp.max(t, axis=0))
                total = total * jnp.exp2(peak - new) + jnp.sum(jnp.exp2(t - new[None]), axis=0)
                peak = new
            top = jnp.max(peak, axis=0, keepdims=True)
            total = jnp.sum(total * jnp.exp2(peak - top), axis=0, keepdims=True)
            col_part[0, k, :, lanes] = top + jnp.log2(total) + bias

    def sum_columns(k):
        for i in range(halves):
            lanes = slice(i * LANES, (i + 1) * LANES)
            total = jnp.zeros((8, LANES), jnp.float32)
            for q in range(chunks):
                at = slice(q * LANES, (q + 1) * LANES)
                t = prod[k, at, lanes] * b_col[at, :]
                total = total + jnp.sum(t.reshape(groups, 8, LANES), axis=0)
            col_part[1, k, :, lanes] = jnp.sum(total, axis=0, keepdims=True)

    def column_pass(iteration, visit):
        def one(step, carry):
            k = peer(step)
            visit(k)
            pltpu.make_async_remote_copy(
                src_ref=col_part.at[iteration, k],
                dst_ref=col_in.at[iteration, step],
                send_sem=col_send.at[iteration],
                recv_sem=col_recv.at[iteration],
                device_id={"tile": k},
                device_id_type=MESH,
            ).start()
            return carry

        lax.fori_loop(0, TILES - 1, one, 0)
        visit(me)
        col_in[iteration, TILES - 1] = col_part[iteration, me]
        view = col_in.at[iteration, pl.ds(0, TILES - 1)]
        pltpu.make_async_copy(view, view, col_recv.at[iteration]).wait()
        return col_in[iteration]

    parts = column_pass(0, log_columns)
    peak = jnp.max(parts, axis=0)
    total = jnp.sum(jnp.exp2(parts - peak[None]), axis=0)
    a = LOG2E * col_logw[...] - (peak + jnp.log2(total))
    a_all[1, me] = a
    send_potential(1)
    wait_potential(1)

    def spread(k, carry):
        a_wide[k] = jnp.broadcast_to(a_all[1, k] + bias_of(k), (8, shard))
        return carry

    lax.fori_loop(0, TILES, spread, 0)
    step_rows = 16

    def plan_rows(step, carry):
        at = pl.ds(pl.multiple_of(step * step_rows, step_rows), step_rows)
        total = jnp.zeros((step_rows // 8, 8, LANES), jnp.float32)
        for k in range(TILES):
            t = jnp.exp2(prod[k, at, :].reshape(step_rows // 8, 8, shard) + a_wide[k][None])
            prod[k, at, :] = t.reshape(step_rows, shard)
            total = total + sum(t[:, :, i * LANES : (i + 1) * LANES] for i in range(halves))
        s_run[at, :] = total.reshape(step_rows, LANES)
        return carry

    lax.fori_loop(0, rows // step_rows, plan_rows, 0)
    for q in range(chunks):
        at = slice(q * LANES, (q + 1) * LANES)
        row_part[1, rep, q : q + 1, :] = jnp.sum(s_run[at, :].T, axis=0, keepdims=True)
    total = sum(exchange_rows(1))
    scale = jnp.exp2(LOG2E * row_logw[...]) / total
    spread_rows(scale)
    b = b + LOG2E * row_logw[...] - jnp.log2(total)

    total = jnp.sum(column_pass(1, sum_columns), axis=0)
    a = a + LOG2E * col_logw[...] - jnp.log2(total)

    row_out[...] = row_sq[...] / depth + dual_scale * b
    col_out[...] = own_sq / depth + dual_scale * a

    view = tgt.at[pl.ds(0, TILES - 1)]
    pltpu.make_async_copy(view, view, gather_send.at[0]).wait()
    for iteration in range(2):
        view = a_all.at[iteration, pl.ds(0, TILES - 1)]
        pltpu.make_async_copy(view, view, a_send.at[iteration]).wait()
        view = row_part.at[iteration, pl.ds(0, REPS - 1)]
        pltpu.make_async_copy(view, view, row_send.at[iteration]).wait()
        view = col_part.at[iteration, pl.ds(0, TILES - 1)]
        pltpu.make_async_copy(view, view, col_send.at[iteration]).wait()


def per_device(source, target, row_logw, col_logw, support):
    rows, depth = source.shape
    shard = target.shape[0]
    vmem = pl.BlockSpec(memory_space=pltpu.VMEM)
    f32 = jnp.float32
    row_dual, col_dual = pl.pallas_call(
        kernel,
        out_shape=(
            jax.ShapeDtypeStruct((rows // LANES, LANES), f32),
            jax.ShapeDtypeStruct((1, shard), f32),
        ),
        in_specs=[pl.BlockSpec(memory_space=pl.ANY)] * 5,
        out_specs=(vmem, vmem),
        scratch_shapes=[
            pltpu.VMEM((rows, depth), source.dtype),
            pltpu.VMEM((TILES, shard, depth), target.dtype),
            pltpu.VMEM((rows // LANES, LANES), f32),
            pltpu.VMEM((1, shard), f32),
            pltpu.SMEM(support.shape, support.dtype),
            pltpu.VMEM((TILES, rows, shard), f32),
            pltpu.VMEM((2, rows, shard), f32),
            pltpu.VMEM((2, rows, shard), f32),
            pltpu.VMEM((rows, LANES), f32),
            pltpu.VMEM((rows, LANES), f32),
            pltpu.VMEM((rows, LANES), f32),
            pltpu.VMEM((2, TILES, 1, shard), f32),
            pltpu.VMEM((TILES, 8, shard), f32),
            pltpu.VMEM((rows // LANES, LANES), f32),
            pltpu.VMEM((2, REPS, rows // LANES, LANES), f32),
            pltpu.VMEM((2, TILES, 1, shard), f32),
            pltpu.VMEM((2, TILES, 1, shard), f32),
            pltpu.SemaphoreType.DMA((5,)),
            pltpu.SemaphoreType.DMA((1,)),
            pltpu.SemaphoreType.DMA((TILES,)),
            pltpu.SemaphoreType.DMA((2,)),
            pltpu.SemaphoreType.DMA((2,)),
            pltpu.SemaphoreType.DMA((2,)),
            pltpu.SemaphoreType.DMA((2,)),
            pltpu.SemaphoreType.DMA((2,)),
            pltpu.SemaphoreType.DMA((2,)),
        ],
        compiler_params=pltpu.CompilerParams(
            collective_id=0, has_side_effects=True, vmem_limit_bytes=63 * 1024 * 1024
        ),
        name="sinkhorn",
    )(
        source,
        target,
        row_logw.reshape(rows // LANES, LANES),
        col_logw.reshape(1, shard),
        support,
    )
    return row_dual.reshape(rows), col_dual.reshape(shard)


def solution(mesh):
    placed = (P("tile", None), P(("rep", "tile"), None), P("tile"), P(("rep", "tile")), P())
    return jax.shard_map(
        per_device,
        mesh=mesh,
        in_specs=placed,
        out_specs=(P("tile"), P(("rep", "tile"))),
        check_vma=False,
    )
```

time: 90.6 us -> 77.2 us (0.85)
  Pallas kernels: 84.5 us -> 74.5 us
  local copies, waits for them, and re-layouts: 5.18 us -> 1.87 us
    pallas_call x1, Pallas kernels: 84.5 us -> 74.5 us  [per_device(): pl.pallas_call(kernel, out_shape=(jax.ShapeDtypeStruct((rows // LANES, LA...]
    unnamed x12 -> x6, local copies, waits for them, and re-layouts: 5.18 us -> 1.87 us
where the time goes in v2:
time: 77.2 us; the launch traced here: 77 us
  Pallas kernels  74.5 us (97%)
  local copies, waits for them, and re-layouts  1.87 us (2%)
    pallas_call x1, Pallas kernels, per_device(): pl.pallas_call(kernel, out_shape=(jax.ShapeDtypeStruct((rows // LANES, LA...  74.5 us
    unnamed x6, local copies, waits for them, and re-layouts  1.87 us

profile of v2, /device:TPU:1, one launch (start us, length us, event | category | flops | bytes accessed | tf_op | source)
XLA Modules:
  0.0 77.0 jit_solution(10737705428375473124)
XLA Ops:
  0.6 74.5 %sinkhorn.1 = (f32[8,128]{1,0:T(8,128)}, f32[1,256]{1,0:T(1,128)}) custom-call(bf16[1024,256]{1,0:T(8,128)(2,1)} %source_hbm.1, bf16[256,256]{1,0:T(8,128)(2,1)} %target_hbm.1, f32[8,128]{1,0:T(8,128)} %bitcast.4, f32[1,256]{1,0:T(1,128)} %bitcast.6, s32[32,32]{1,0:T(8,128)} %support_hbm.1), custom_call_target="tpu_custom_call" | custom-call | tf_op jit(solution)/shard_map/sinkhorn/pallas_call | solution.py:388
  75.1 0.0 copy-start
  75.2 0.7 copy-done
  75.8 0.0 copy-start.1
  75.8 0.6 copy.9
  76.4 0.0 copy-done.1
  76.5 0.6 copy.10
Async XLA Ops:
  75.1 0.7 copy-start
  75.8 0.6 copy-start.1

commit v3 on v2

v3 whole, which is shorter than its diff:
```python
import functools
import math

import jax
import jax.numpy as jnp
from jax import lax
from jax.experimental import pallas as pl
from jax.experimental.pallas import tpu as pltpu
from jax.sharding import PartitionSpec as P

MESH = pl.DeviceIdType.MESH
EPS = 0.1
NEG = -1e30
LOG2E = 1.0 / math.log(2.0)
LN2 = math.log(2.0)
NX = 4
TILES = 2 * NX * NX
GROUP = TILES // 2
REPS = 4
LANES = 128


def kernel(
    source_hbm,
    target_hbm,
    row_logw_hbm,
    col_logw_hbm,
    support_hbm,
    row_out,
    col_out,
    src,
    tgt,
    row_logw,
    col_logw,
    support,
    prod,
    stage_a,
    stage_b,
    m_run,
    s_run,
    b_col,
    b_keep,
    a_all,
    a_wide,
    row_sq,
    row_part,
    col_part,
    col_in,
    local_sem,
    logw_sem,
    src_send,
    src_recv,
    gather_send,
    gather_recv,
    a_send,
    a_recv,
    row_send,
    row_recv,
    col_send,
    col_recv,
):
    rows = src.shape[1]
    shard = col_logw.shape[1]
    depth = src.shape[2]
    blocks = TILES * shard // rows
    per_block = TILES // blocks
    chunks = rows // LANES
    halves = shard // LANES
    me = lax.axis_index("tile")
    rep = lax.axis_index("rep")
    core = me % 2
    x = me // (2 * NX)
    z = (me // 2) % NX
    half = x // 2
    xl = x % 2
    base = half * GROUP
    slot = me - base
    partner = me + 1 - 2 * core
    across = ((NX - 1 - x) * NX + z) * 2 + core
    row_tiles = [me * (1 - half) + across * half, across * (1 - half) + me * half]
    score_scale = 2.0 * LOG2E / (depth * EPS)
    square_scale = LOG2E / (depth * EPS)
    dual_scale = EPS * LN2

    zs = [(z + i) % NX for i in range(NX)]
    xls = [xl, 1 - xl]

    def place(dx, dz, of):
        return (xls[dx] * NX + zs[dz]) * 2 + of

    def mine(dx, dz):
        return place(dx, dz, core)

    def theirs(dx, dz):
        return place(dx, dz, 1 - core)

    def chip(step):
        m = NX - 1 - step % NX
        dz = m + m // 2 - 2 * (m // 3)
        return (((xl + 1 - step // NX) % 2) * NX + (z + dz) % NX) * 2

    def each_chip(visit):
        def one(step, at):
            visit(step, at)
            return chip(step + 1)

        lax.fori_loop(0, GROUP // 2 - 1, one, chip(0))

    def to_others(start):
        def both(step, at):
            start(2 * step, at + core)
            start(2 * step + 1, at + 1 - core)

        each_chip(both)
        start(GROUP - 2, slot + 1 - 2 * core)

    row_peers = [{"tile": me, "rep": (rep + i) % REPS} for i in range(1, REPS)]
    row_peers += [{"tile": across, "rep": (rep + i) % REPS} for i in range(REPS)]

    loads = [
        pltpu.make_async_copy(target_hbm, tgt.at[slot, pl.ds(0, shard)], local_sem.at[0]),
        pltpu.make_async_copy(source_hbm, src.at[half], local_sem.at[1]),
        pltpu.make_async_copy(support_hbm, support, local_sem.at[2]),
        pltpu.make_async_copy(row_logw_hbm, row_logw.at[half], local_sem.at[3]),
        pltpu.make_async_copy(col_logw_hbm, col_logw, local_sem.at[4]),
    ]
    for load in loads:
        load.start()

    barrier = pltpu.get_barrier_semaphore()

    def greet(message, at):
        pl.semaphore_signal(
            barrier, inc=1, device_id={"tile": base + at}, device_id_type=MESH
        )

    to_others(greet)
    for peer in row_peers:
        pl.semaphore_signal(barrier, inc=1, device_id=peer, device_id_type=MESH)

    loads[0].wait()
    own = tgt[slot, :shard].astype(jnp.float32)
    own_sq = jnp.sum((own * own).T, axis=0, keepdims=True)
    rest = -square_scale * own_sq
    parts = []
    for _ in range(3):
        parts.append(rest.astype(jnp.bfloat16))
        rest = rest - parts[-1].astype(jnp.float32)
    extra = tgt.shape[1] - shard
    tgt[slot, shard:] = jnp.concatenate(
        parts + [jnp.zeros((extra - 3, depth), jnp.bfloat16)], axis=0
    )

    pl.semaphore_wait(barrier, GROUP - 1 + len(row_peers))

    quarter = rows // REPS

    def rows_at(i):
        return pl.ds(pl.multiple_of((rep + i) % REPS * quarter, quarter), quarter)

    def send_rows(i, sem):
        pltpu.make_async_remote_copy(
            src_ref=source_hbm.at[rows_at(i)],
            dst_ref=src.at[half, rows_at(i)],
            send_sem=src_send.at[sem],
            recv_sem=src_recv.at[(rep + i) % REPS],
            device_id={"tile": across},
            device_id_type=MESH,
        ).start()

    def wait_rows(i):
        view = src.at[1 - half, rows_at(i)]
        pltpu.make_async_copy(view, view, src_recv.at[(rep + i) % REPS]).wait()

    def pass_rows(to):
        view = src.at[1 - half, rows_at(0)]
        pltpu.make_async_remote_copy(
            src_ref=view,
            dst_ref=view,
            send_sem=src_send.at[1],
            recv_sem=src_recv.at[rep],
            device_id={"rep": (rep + to) % REPS},
            device_id_type=MESH,
        ).start()

    def send_shard(k, to):
        pltpu.make_async_remote_copy(
            src_ref=tgt.at[k],
            dst_ref=tgt.at[k],
            send_sem=gather_send.at[0],
            recv_sem=gather_recv.at[k],
            device_id={"tile": base + to},
            device_id_type=MESH,
        ).start()

    def wait_shard(k):
        pltpu.make_async_copy(tgt.at[k], tgt.at[k], gather_recv.at[k]).wait()

    partner_slot = slot + 1 - 2 * core
    send_rows(0, 0)
    send_shard(slot, mine(1, 0))
    for dz in (1, 3, 2):
        send_shard(slot, mine(0, dz))
    send_shard(slot, partner_slot)
    logw_copy = pltpu.make_async_remote_copy(
        src_ref=row_logw_hbm,
        dst_ref=row_logw.at[half],
        send_sem=logw_sem.at[0],
        recv_sem=logw_sem.at[1],
        device_id={"tile": across},
        device_id_type=MESH,
    )
    logw_copy.start()

    def share_potential():
        def start(message, to):
            pltpu.make_async_remote_copy(
                src_ref=a_all.at[slot],
                dst_ref=a_all.at[slot],
                send_sem=a_send.at[0],
                recv_sem=a_recv.at[0],
                device_id={"tile": base + to},
                device_id_type=MESH,
            ).start()

        to_others(start)
        view = a_all.at[pl.ds(0, GROUP - 1)]
        pltpu.make_async_copy(view, view, a_recv.at[0]).wait()

    def bias_of(i, k):
        tile = row_tiles[0] * (1 - i) + row_tiles[1] * i
        live = support[tile, rep * blocks + (base + k) // per_block]
        return (1.0 - live.astype(jnp.float32)) * NEG

    for load in loads[1:]:
        load.wait()

    m_run[...] = jnp.full(m_run.shape, NEG, jnp.float32)
    s_run[...] = jnp.zeros(s_run.shape, jnp.float32)
    for q in range(chunks):
        cells = src[half, q * LANES : (q + 1) * LANES, :].astype(jnp.float32)
        sq = cells * cells
        sq = sum(sq[:, i * LANES : (i + 1) * LANES] for i in range(depth // LANES))
        row_sq[q : q + 1, :] = jnp.sum(sq.T, axis=0, keepdims=True)

    view = src.at[0, pl.ds(0, quarter)]
    pltpu.make_async_copy(view, view, src_send.at[0]).wait()
    send_rows(2, 1)

    def against(left, right):
        return lax.dot_general(
            left, right, (((1,), (1,)), ((), ())), preferred_element_type=jnp.float32
        )

    def products(i, pair, stage):
        for n, k in enumerate(pair):
            for r in range(0, rows, 512):
                stage[n, r : r + 512, :] = against(src[i, r : r + 512, :], tgt[k, :shard])

    def column_term(i, k):
        parts = tgt[k, shard:].astype(jnp.float32)
        return parts[0:1] + parts[1:2] + parts[2:3] + bias_of(i, k)

    def update(i, pair, stage, terms):
        step = 32
        for r in range(0, rows, step):
            at = slice(r, r + step)
            t = []
            for n, k in enumerate(pair):
                p = stage[n, at, :] * score_scale
                prod[k, i, at, :] = p
                t.extend(
                    p[:, h * LANES : (h + 1) * LANES] + terms[n][:, h * LANES : (h + 1) * LANES]
                    for h in range(halves)
                )
            old = m_run[i, at, :]
            new = functools.reduce(jnp.maximum, t, old)
            m_run[i, at, :] = new
            s_run[i, at, :] = s_run[i, at, :] * jnp.exp2(old - new) + sum(
                jnp.exp2(v - new) for v in t
            )

    def handle(entry):
        whose, dx, dz = entry
        if whose == "theirs":
            k = theirs(dx, dz)
            wait_shard(k)
            return k
        k = mine(dx, dz)
        if dx == 0 and dz == 0:
            return k
        wait_shard(k)
        if dx == 1 and dz == 0:

            @pl.when(core == 0)
            def _():
                for step in (1, 3, 2):
                    send_shard(k, mine(0, step))

        elif dx == 0:

            @pl.when(core == 1)
            def _():
                send_shard(k, mine(1, 0))

        send_shard(k, partner_slot)
        return k

    def m(dx, dz):
        return ("mine", dx, dz)

    def t(dx, dz):
        return ("theirs", dx, dz)

    pairs = [
        (m(0, 0), t(0, 0)),
        (m(1, 0), m(0, 1)),
        (m(0, 3), m(0, 2)),
        (t(1, 0), t(0, 1)),
        (t(0, 3), t(0, 2)),
        (m(1, 1), m(1, 3)),
        (t(1, 1), t(1, 3)),
        (m(1, 2), t(1, 2)),
    ]
    steps = [(0, 0), (1, 0), (2, 0), (3, 0), (4, 0), (0, 1), (1, 1), (5, 0)]
    steps += [(2, 1), (3, 1), (6, 0), (4, 1), (5, 1), (7, 0), (6, 1), (7, 1)]
    stages = (stage_a, stage_b)
    ready = {}
    before = None
    for n in range(len(steps) + 1):
        now = None
        if n < len(steps):
            which, other = steps[n]
            if which not in ready:
                ready[which] = [handle(entry) for entry in pairs[which]]
            if n == 1:
                wait_rows(0)
                pass_rows(1)
                pass_rows(3)
            if n == 5:
                for i in (2, 1, 3):
                    wait_rows(i)
            i = (1 - half) if other else half
            now = (i, ready[which])
        if before is not None:
            terms = [column_term(before[0], k) for k in before[1]]
        if now is not None:
            products(now[0], now[1], stages[n % 2])
        if before is not None:
            update(before[0], before[1], stages[(n + 1) % 2], terms)
        before = now

    row_slot = half * REPS + rep

    def exchange_rows(iteration):
        for peer in row_peers:
            pltpu.make_async_remote_copy(
                src_ref=row_part.at[iteration, row_slot],
                dst_ref=row_part.at[iteration, row_slot],
                send_sem=row_send.at[iteration],
                recv_sem=row_recv.at[iteration],
                device_id=peer,
                device_id_type=MESH,
            ).start()
        view = row_part.at[iteration, pl.ds(0, len(row_peers))]
        pltpu.make_async_copy(view, view, row_recv.at[iteration]).wait()
        return [row_part[iteration, i] for i in range(2 * REPS)]

    def spread_rows(values):
        for i in range(2):
            for q in range(chunks):
                b_col[i, q * LANES : (q + 1) * LANES, :] = jnp.broadcast_to(
                    values[i, q : q + 1, :], (LANES, LANES)
                ).T

    for i in range(2):
        for q in range(chunks):
            at = slice(q * LANES, (q + 1) * LANES)
            m = m_run[i, at, :].T
            s = s_run[i, at, :].T
            peak = jnp.max(m, axis=0, keepdims=True)
            total = jnp.sum(s * jnp.exp2(m - peak), axis=0, keepdims=True)
            row_part[0, row_slot, i, q : q + 1, :] = peak + jnp.log2(total)
    parts = exchange_rows(0)
    peak = functools.reduce(jnp.maximum, parts)
    total = sum(jnp.exp2(v - peak) for v in parts)
    logw_copy.wait()
    b = LOG2E * row_logw[...] - (peak + jnp.log2(total))
    spread_rows(b)

    groups = LANES // 8

    def tree(op, v):
        while v.shape[0] > 1:
            n = v.shape[0] // 2
            v = op(v[:n], v[n:])
        return v[0]

    def lane_tiles(v):
        return [v[..., i * LANES : (i + 1) * LANES] for i in range(halves)]

    def log_columns(pair):
        tiles = [(k, slice(i * LANES, (i + 1) * LANES)) for k in pair for i in range(halves)]
        parts = []
        for block in range(2):
            biases = [bias_of(block, k) for k in pair]
            peaks = [jnp.full((8, LANES), NEG, jnp.float32)] * len(tiles)
            totals = [jnp.zeros((8, LANES), jnp.float32)] * len(tiles)
            for q in range(chunks):
                at = slice(q * LANES, (q + 1) * LANES)
                row_term = b_col[block, at, :]
                for n, (k, lanes) in enumerate(tiles):
                    t = prod[k, block, at, lanes] + row_term
                    prod[k, block, at, lanes] = t
                    t = t.reshape(groups, 8, LANES)
                    new = jnp.maximum(peaks[n], tree(jnp.maximum, t))
                    totals[n] = totals[n] * jnp.exp2(peaks[n] - new) + tree(
                        jnp.add, jnp.exp2(t - new[None])
                    )
                    peaks[n] = new
            for n in range(len(tiles)):
                top = jnp.max(peaks[n], axis=0, keepdims=True)
                total = jnp.sum(totals[n] * jnp.exp2(peaks[n] - top), axis=0, keepdims=True)
                parts.append(top + jnp.log2(total) + biases[n // halves])
        for n, (k, lanes) in enumerate(tiles):
            one, two = parts[n], parts[n + len(tiles)]
            top = jnp.maximum(one, two)
            col_part[0, k, :, lanes] = top + jnp.log2(jnp.exp2(one - top) + jnp.exp2(two - top))

    def sum_columns(pair):
        tiles = [(k, slice(i * LANES, (i + 1) * LANES)) for k in pair for i in range(halves)]
        totals = [jnp.zeros((4, 8, LANES), jnp.float32)] * len(tiles)
        few = 64
        for block in range(2):
            for r in range(0, rows, few):
                at = slice(r, r + few)
                row_term = b_col[block, at, :]
                for n, (k, lanes) in enumerate(tiles):
                    t = (prod[k, block, at, lanes] * row_term).reshape(2, 4, 8, LANES)
                    totals[n] = totals[n] + (t[0] + t[1])
        for n, (k, lanes) in enumerate(tiles):
            col_part[1, k, :, lanes] = jnp.sum(tree(jnp.add, totals[n]), axis=0, keepdims=True)

    def column_pass(iteration, visit):
        def start(message, k):
            pltpu.make_async_remote_copy(
                src_ref=col_part.at[iteration, k],
                dst_ref=col_in.at[iteration, message],
                send_sem=col_send.at[iteration],
                recv_sem=col_recv.at[iteration],
                device_id={"tile": base + k},
                device_id_type=MESH,
            ).start()

        def both(step, at):
            visit((at, at + 1))
            start(2 * step, at + core)
            start(2 * step + 1, at + 1 - core)

        each_chip(both)
        visit((slot - core, slot - core + 1))
        start(GROUP - 2, partner_slot)
        col_in[iteration, GROUP - 1] = col_part[iteration, slot]
        view = col_in.at[iteration, pl.ds(0, GROUP - 1)]
        pltpu.make_async_copy(view, view, col_recv.at[iteration]).wait()
        return col_in[iteration]

    parts = column_pass(0, log_columns)
    peak = jnp.max(parts, axis=0)
    total = jnp.sum(jnp.exp2(parts - peak[None]), axis=0)
    a = LOG2E * col_logw[...] - (peak + jnp.log2(total))
    a_all[slot] = a
    share_potential()

    def spread(k, carry):
        for i in range(2):
            a_wide[i, k] = jnp.broadcast_to(a_all[k] + bias_of(i, k), (8, shard))
        return carry

    lax.fori_loop(0, GROUP, spread, 0)
    step_rows = 32

    def plan_rows(step, carry):
        block = step // (rows // step_rows)
        at = pl.ds(
            pl.multiple_of(step % (rows // step_rows) * step_rows, step_rows), step_rows
        )
        totals = [jnp.zeros((step_rows // 8, 8, LANES), jnp.float32)] * 2
        for k in range(GROUP):
            t = jnp.exp2(
                prod[k, block, at, :].reshape(step_rows // 8, 8, shard) + a_wide[block, k][None]
            )
            prod[k, block, at, :] = t.reshape(step_rows, shard)
            totals[k % 2] = totals[k % 2] + sum(lane_tiles(t))
        s_run[block, at, :] = sum(totals).reshape(step_rows, LANES)
        return carry

    lax.fori_loop(0, 2 * rows // step_rows, plan_rows, 0)
    for i in range(2):
        for q in range(chunks):
            at = slice(q * LANES, (q + 1) * LANES)
            row_part[1, row_slot, i, q : q + 1, :] = jnp.sum(
                s_run[i, at, :].T, axis=0, keepdims=True
            )
    total = sum(exchange_rows(1))
    scale = jnp.exp2(LOG2E * row_logw[...]) / total
    spread_rows(scale)
    b_keep[...] = b + LOG2E * row_logw[...] - jnp.log2(total)

    total = jnp.sum(column_pass(1, sum_columns), axis=0)
    a = a + LOG2E * col_logw[...] - jnp.log2(total)

    row_out[...] = row_sq[...] / depth + dual_scale * b_keep[half]
    col_out[...] = own_sq / depth + dual_scale * a

    view = tgt.at[pl.ds(0, GROUP - 1)]
    pltpu.make_async_copy(view, view, gather_send.at[0]).wait()
    view = src.at[0, pl.ds(0, 3 * quarter)]
    pltpu.make_async_copy(view, view, src_send.at[1]).wait()
    view = a_all.at[pl.ds(0, GROUP - 1)]
    pltpu.make_async_copy(view, view, a_send.at[0]).wait()
    for iteration in range(2):
        view = row_part.at[iteration, pl.ds(0, len(row_peers))]
        pltpu.make_async_copy(view, view, row_send.at[iteration]).wait()
        view = col_part.at[iteration, pl.ds(0, GROUP - 1)]
        pltpu.make_async_copy(view, view, col_send.at[iteration]).wait()


def per_device(source, target, row_logw, col_logw, support):
    rows, depth = source.shape
    shard = target.shape[0]
    vmem = pl.BlockSpec(memory_space=pltpu.VMEM)
    f32 = jnp.float32
    row_dual, col_dual = pl.pallas_call(
        kernel,
        out_shape=(
            jax.ShapeDtypeStruct((rows // LANES, LANES), f32),
            jax.ShapeDtypeStruct((1, shard), f32),
        ),
        in_specs=[pl.BlockSpec(memory_space=pl.ANY)] * 5,
        out_specs=(vmem, vmem),
        scratch_shapes=[
            pltpu.VMEM((2, rows, depth), source.dtype),
            pltpu.VMEM((GROUP, shard + 16, depth), target.dtype),
            pltpu.VMEM((2, rows // LANES, LANES), f32),
            pltpu.VMEM((1, shard), f32),
            pltpu.SMEM(support.shape, support.dtype),
            pltpu.VMEM((GROUP, 2, rows, shard), f32),
            pltpu.VMEM((2, rows, shard), f32),
            pltpu.VMEM((2, rows, shard), f32),
            pltpu.VMEM((2, rows, LANES), f32),
            pltpu.VMEM((2, rows, LANES), f32),
            pltpu.VMEM((2, rows, LANES), f32),
            pltpu.VMEM((2, rows // LANES, LANES), f32),
            pltpu.VMEM((GROUP, 1, shard), f32),
            pltpu.VMEM((2, GROUP, 8, shard), f32),
            pltpu.VMEM((rows // LANES, LANES), f32),
            pltpu.VMEM((2, 2 * REPS, 2, rows // LANES, LANES), f32),
            pltpu.VMEM((2, GROUP, 1, shard), f32),
            pltpu.VMEM((2, GROUP, 1, shard), f32),
            pltpu.SemaphoreType.DMA((5,)),
            pltpu.SemaphoreType.DMA((2,)),
            pltpu.SemaphoreType.DMA((2,)),
            pltpu.SemaphoreType.DMA((REPS,)),
            pltpu.SemaphoreType.DMA((1,)),
            pltpu.SemaphoreType.DMA((GROUP,)),
            pltpu.SemaphoreType.DMA((1,)),
            pltpu.SemaphoreType.DMA((1,)),
            pltpu.SemaphoreType.DMA((2,)),
            pltpu.SemaphoreType.DMA((2,)),
            pltpu.SemaphoreType.DMA((2,)),
            pltpu.SemaphoreType.DMA((2,)),
        ],
        compiler_params=pltpu.CompilerParams(
            collective_id=0, has_side_effects=True, vmem_limit_bytes=63 * 1024 * 1024
        ),
        name="sinkhorn",
    )(
        source,
        target,
        row_logw.reshape(rows // LANES, LANES),
        col_logw.reshape(1, shard),
        support,
    )
    return row_dual.reshape(rows), col_dual.reshape(shard)


def solution(mesh):
    placed = (P("tile", None), P(("rep", "tile"), None), P("tile"), P(("rep", "tile")), P())
    return jax.shard_map(
        per_device,
        mesh=mesh,
        in_specs=placed,
        out_specs=(P("tile"), P(("rep", "tile"))),
        check_vma=False,
    )
```

time: 77.2 us -> 72.5 us (0.939)
  Pallas kernels: 74.5 us -> 69.8 us
    pallas_call x1, Pallas kernels: 74.5 us -> 69.8 us  [per_device(): pl.pallas_call(kernel, out_shape=(jax.ShapeDtypeStruct((rows // LANES, LA...]
where the time goes in v3:
time: 72.5 us; the launch traced here: 72.4 us
  Pallas kernels  69.8 us (96%)
  local copies, waits for them, and re-layouts  1.87 us (3%)
    pallas_call x1, Pallas kernels, per_device(): pl.pallas_call(kernel, out_shape=(jax.ShapeDtypeStruct((rows // LANES, LA...  69.8 us
    unnamed x6, local copies, waits for them, and re-layouts  1.87 us

profile of v3, /device:TPU:1, one launch (start us, length us, event | category | flops | bytes accessed | tf_op | source)
XLA Modules:
  0.0 72.4 jit_solution(11957488750213669467)
XLA Ops:
  0.6 69.8 %sinkhorn.1 = (f32[8,128]{1,0:T(8,128)}, f32[1,256]{1,0:T(1,128)}) custom-call(bf16[1024,256]{1,0:T(8,128)(2,1)} %source_hbm.1, bf16[256,256]{1,0:T(8,128)(2,1)} %target_hbm.1, f32[8,128]{1,0:T(8,128)} %bitcast.4, f32[1,256]{1,0:T(1,128)} %bitcast.6, s32[32,32]{1,0:T(8,128)} %support_hbm.1), custom_call_target="tpu_custom_call" | custom-call | tf_op jit(solution)/shard_map/sinkhorn/pallas_call | solution.py:534
  70.5 0.0 copy-start
  70.5 0.7 copy-done
  71.2 0.0 copy-start.1
  71.2 0.6 copy.9
  71.8 0.0 copy-done.1
  71.8 0.6 copy.10
Async XLA Ops:
  70.5 0.7 copy-start
  71.2 0.6 copy-start.1

commit v4 on v3

--- a/solution.py
+++ b/solution.py
@@ -114,6 +114,15 @@
         each_chip(both)
         start(GROUP - 2, slot + 1 - 2 * core)
 
+    def reached(j, c):
+        return (j + 16 - c) // 16
+
+    def pair_at(p):
+        turn = (p + 1) % 3
+        dz = (1 + 2 * turn - 3 * (turn // 2)) * reached(p, 2)
+        dx = reached(p, 1) - reached(p, 2) + reached(p, 5)
+        return (((xl + dx) % 2) * NX + (z + dz) % NX) * 2
+
     row_peers = [{"tile": me, "rep": (rep + i) % REPS} for i in range(1, REPS)]
     row_peers += [{"tile": across, "rep": (rep + i) % REPS} for i in range(REPS)]
 
@@ -214,18 +223,24 @@
 
     def share_potential():
         def start(message, to):
+            step = message // 2
+            near = reached(step, 3) - reached(step, 4) + reached(step, 5)
             pltpu.make_async_remote_copy(
                 src_ref=a_all.at[slot],
                 dst_ref=a_all.at[slot],
                 send_sem=a_send.at[0],
-                recv_sem=a_recv.at[0],
+                recv_sem=a_recv.at[1 - near],
                 device_id={"tile": base + to},
                 device_id_type=MESH,
             ).start()
 
         to_others(start)
-        view = a_all.at[pl.ds(0, GROUP - 1)]
-        pltpu.make_async_copy(view, view, a_recv.at[0]).wait()
+
+    near_messages = 7
+
+    def wait_potential(far):
+        view = a_all.at[pl.ds(0, GROUP - 1 - near_messages if far else near_messages)]
+        pltpu.make_async_copy(view, view, a_recv.at[far]).wait()
 
     def bias_of(i, k):
         tile = row_tiles[0] * (1 - i) + row_tiles[1] * i
@@ -280,113 +295,130 @@
                 jnp.exp2(v - new) for v in t
             )
 
-    def handle(entry):
-        whose, dx, dz = entry
-        if whose == "theirs":
-            k = theirs(dx, dz)
-            wait_shard(k)
-            return k
-        k = mine(dx, dz)
-        if dx == 0 and dz == 0:
-            return k
+    def receive(p):
+        k = pair_at(p) + core
         wait_shard(k)
-        if dx == 1 and dz == 0:
-
-            @pl.when(core == 0)
-            def _():
-                for step in (1, 3, 2):
-                    send_shard(k, mine(0, step))
-
-        elif dx == 0:
-
-            @pl.when(core == 1)
-            def _():
-                send_shard(k, mine(1, 0))
+
+        @pl.when(core * 8 + p == 1)
+        def _():
+            for dz in (1, 3, 2):
+                send_shard(k, mine(0, dz))
+
+        @pl.when(core * reached(p, 2) * (1 - reached(p, 5)) == 1)
+        def _():
+            send_shard(k, mine(1, 0))
 
         send_shard(k, partner_slot)
-        return k
-
-    def m(dx, dz):
-        return ("mine", dx, dz)
-
-    def t(dx, dz):
-        return ("theirs", dx, dz)
-
-    pairs = [
-        (m(0, 0), t(0, 0)),
-        (m(1, 0), m(0, 1)),
-        (m(0, 3), m(0, 2)),
-        (t(1, 0), t(0, 1)),
-        (t(0, 3), t(0, 2)),
-        (m(1, 1), m(1, 3)),
-        (t(1, 1), t(1, 3)),
-        (m(1, 2), t(1, 2)),
-    ]
-    steps = [(0, 0), (1, 0), (2, 0), (3, 0), (4, 0), (0, 1), (1, 1), (5, 0)]
-    steps += [(2, 1), (3, 1), (6, 0), (4, 1), (5, 1), (7, 0), (6, 1), (7, 1)]
-    stages = (stage_a, stage_b)
-    ready = {}
-    before = None
-    for n in range(len(steps) + 1):
-        now = None
-        if n < len(steps):
-            which, other = steps[n]
-            if which not in ready:
-                ready[which] = [handle(entry) for entry in pairs[which]]
-            if n == 1:
-                wait_rows(0)
-                pass_rows(1)
-                pass_rows(3)
-            if n == 5:
-                for i in (2, 1, 3):
-                    wait_rows(i)
-            i = (1 - half) if other else half
-            now = (i, ready[which])
-        if before is not None:
-            terms = [column_term(before[0], k) for k in before[1]]
-        if now is not None:
-            products(now[0], now[1], stages[n % 2])
-        if before is not None:
-            update(before[0], before[1], stages[(n + 1) % 2], terms)
-        before = now
+
+    def receive_theirs(p):
+        wait_shard(pair_at(p) + 1 - core)
+
+    def rows_of(other):
+        return half + other * (1 - 2 * half)
+
+    def step_at(n):
+        late = reached(n, 4)
+        par = reached(n, 8) * (1 - half) + (late - reached(n, 12)) * half
+        p = n - 8 * reached(n, 8) * (1 - half) - 4 * (late + reached(n, 12)) * half
+        at = pair_at(p - reached(n, 16))
+        return half + par * (1 - 2 * half), (at, at + 1)
 
     row_slot = half * REPS + rep
 
-    def exchange_rows(iteration):
+    def send_row_sums(iteration, block):
         for peer in row_peers:
             pltpu.make_async_remote_copy(
-                src_ref=row_part.at[iteration, row_slot],
-                dst_ref=row_part.at[iteration, row_slot],
-                send_sem=row_send.at[iteration],
-                recv_sem=row_recv.at[iteration],
+                src_ref=row_part.at[iteration, block, row_slot],
+                dst_ref=row_part.at[iteration, block, row_slot],
+                send_sem=row_send.at[iteration, block],
+                recv_sem=row_recv.at[iteration, block],
                 device_id=peer,
                 device_id_type=MESH,
             ).start()
-        view = row_part.at[iteration, pl.ds(0, len(row_peers))]
-        pltpu.make_async_copy(view, view, row_recv.at[iteration]).wait()
-        return [row_part[iteration, i] for i in range(2 * REPS)]
-
-    def spread_rows(values):
-        for i in range(2):
-            for q in range(chunks):
-                b_col[i, q * LANES : (q + 1) * LANES, :] = jnp.broadcast_to(
-                    values[i, q : q + 1, :], (LANES, LANES)
-                ).T
-
-    for i in range(2):
+
+    def take_row_sums(iteration, block):
+        view = row_part.at[iteration, block, pl.ds(0, len(row_peers))]
+        pltpu.make_async_copy(view, view, row_recv.at[iteration, block]).wait()
+        return [row_part[iteration, block, i] for i in range(2 * REPS)]
+
+    def spread_rows(block, values):
+        for q in range(chunks):
+            b_col[block, q * LANES : (q + 1) * LANES, :] = jnp.broadcast_to(
+                values[q : q + 1, :], (LANES, LANES)
+            ).T
+
+    def fold_log_rows(block):
         for q in range(chunks):
             at = slice(q * LANES, (q + 1) * LANES)
-            m = m_run[i, at, :].T
-            s = s_run[i, at, :].T
+            m = m_run[block, at, :].T
+            s = s_run[block, at, :].T
             peak = jnp.max(m, axis=0, keepdims=True)
             total = jnp.sum(s * jnp.exp2(m - peak), axis=0, keepdims=True)
-            row_part[0, row_slot, i, q : q + 1, :] = peak + jnp.log2(total)
-    parts = exchange_rows(0)
-    peak = functools.reduce(jnp.maximum, parts)
-    total = sum(jnp.exp2(v - peak) for v in parts)
+            row_part[0, block, row_slot, q : q + 1, :] = peak + jnp.log2(total)
+        send_row_sums(0, block)
+
+    turns = 8
+    receive_theirs(0)
+    products(*step_at(0), stage_a)
+
+    def turn(j, carry):
+        @pl.when(j == 6)
+        def _():
+            fold_log_rows(0)
+
+        now = step_at(2 * j)
+
+        @pl.when(j == 0)
+        def _():
+            receive(1)
+            wait_rows(0)
+            pass_rows(1)
+            pass_rows(3)
+            receive(2)
+            receive_theirs(1)
+
+        @pl.when(reached(j, 1) * (1 - reached(j, 4)) == 1)
+        def _():
+            @pl.when(j < 3)
+            def _():
+                receive(2 * j + 2)
+
+            receive_theirs(2 * j + 1)
+
+        later = step_at(2 * j + 1)
+        terms = [column_term(now[0], k) for k in now[1]]
+        products(*later, stage_b)
+        update(*now, stage_a, terms)
+
+        now = later
+
+        @pl.when(j < 3)
+        def _():
+            receive(2 * j + 3)
+            receive_theirs(2 * j + 2)
+
+        @pl.when(j == 3 - 2 * half)
+        def _():
+            for i in (2, 1, 3):
+                wait_rows(i)
+
+        later = step_at(2 * j + 2)
+        terms = [column_term(now[0], k) for k in now[1]]
+        products(*later, stage_a)
+        update(*now, stage_b, terms)
+        return carry
+
+    lax.fori_loop(0, turns, turn, 0)
+    fold_log_rows(1)
     logw_copy.wait()
-    b = LOG2E * row_logw[...] - (peak + jnp.log2(total))
-    spread_rows(b)
+
+    def finish_log_rows(block):
+        parts = take_row_sums(0, block)
+        peak = functools.reduce(jnp.maximum, parts)
+        total = sum(jnp.exp2(v - peak) for v in parts)
+        b = LOG2E * row_logw[block] - (peak + jnp.log2(total))
+        b_keep[block] = b
+        spread_rows(block, b)
 
     groups = LANES // 8
 
@@ -399,47 +431,73 @@
     def lane_tiles(v):
         return [v[..., i * LANES : (i + 1) * LANES] for i in range(halves)]
 
-    def log_columns(pair):
-        tiles = [(k, slice(i * LANES, (i + 1) * LANES)) for k in pair for i in range(halves)]
+    def tiles_of(pair):
+        return [(k, slice(i * LANES, (i + 1) * LANES)) for k in pair for i in range(halves)]
+
+    def log_columns(pair, block):
+        tiles = tiles_of(pair)
+        biases = [bias_of(block, k) for k in pair]
+        peaks = [jnp.full((8, LANES), NEG, jnp.float32)] * len(tiles)
+        totals = [jnp.zeros((8, LANES), jnp.float32)] * len(tiles)
+        for q in range(chunks):
+            at = slice(q * LANES, (q + 1) * LANES)
+            row_term = b_col[block, at, :]
+            for n, (k, lanes) in enumerate(tiles):
+                t = prod[k, block, at, lanes] + row_term
+                prod[k, block, at, lanes] = t
+                t = t.reshape(groups, 8, LANES)
+                new = jnp.maximum(peaks[n], tree(jnp.maximum, t))
+                totals[n] = totals[n] * jnp.exp2(peaks[n] - new) + tree(
+                    jnp.add, jnp.exp2(t - new[None])
+                )
+                peaks[n] = new
         parts = []
-        for block in range(2):
-            biases = [bias_of(block, k) for k in pair]
-            peaks = [jnp.full((8, LANES), NEG, jnp.float32)] * len(tiles)
-            totals = [jnp.zeros((8, LANES), jnp.float32)] * len(tiles)
-            for q in range(chunks):
-                at = slice(q * LANES, (q + 1) * LANES)
-                row_term = b_col[block, at, :]
-                for n, (k, lanes) in enumerate(tiles):
-                    t = prod[k, block, at, lanes] + row_term
-                    prod[k, block, at, lanes] = t
-                    t = t.reshape(groups, 8, LANES)
-                    new = jnp.maximum(peaks[n], tree(jnp.maximum, t))
-                    totals[n] = totals[n] * jnp.exp2(peaks[n] - new) + tree(
-                        jnp.add, jnp.exp2(t - new[None])
-                    )
-                    peaks[n] = new
-            for n in range(len(tiles)):
-                top = jnp.max(peaks[n], axis=0, keepdims=True)
-                total = jnp.sum(totals[n] * jnp.exp2(peaks[n] - top), axis=0, keepdims=True)
-                parts.append(top + jnp.log2(total) + biases[n // halves])
-        for n, (k, lanes) in enumerate(tiles):
-            one, two = parts[n], parts[n + len(tiles)]
+        for n in range(len(tiles)):
+            top = jnp.max(peaks[n], axis=0, keepdims=True)
+            total = jnp.sum(totals[n] * jnp.exp2(peaks[n] - top), axis=0, keepdims=True)
+            parts.append(top + jnp.log2(total) + biases[n // halves])
+        return parts
+
+    def log_first(pair):
+        for (k, lanes), part in zip(tiles_of(pair), log_columns(pair, 0)):
+            col_part[0, k, :, lanes] = part
+
+    def log_second(pair):
+        for (k, lanes), two in zip(tiles_of(pair), log_columns(pair, 1)):
+            one = col_part[0, k, :, lanes]
             top = jnp.maximum(one, two)
             col_part[0, k, :, lanes] = top + jnp.log2(jnp.exp2(one - top) + jnp.exp2(two - top))
 
-    def sum_columns(pair):
-        tiles = [(k, slice(i * LANES, (i + 1) * LANES)) for k in pair for i in range(halves)]
-        totals = [jnp.zeros((4, 8, LANES), jnp.float32)] * len(tiles)
-        few = 64
-        for block in range(2):
-            for r in range(0, rows, few):
-                at = slice(r, r + few)
-                row_term = b_col[block, at, :]
-                for n, (k, lanes) in enumerate(tiles):
-                    t = (prod[k, block, at, lanes] * row_term).reshape(2, 4, 8, LANES)
-                    totals[n] = totals[n] + (t[0] + t[1])
-        for n, (k, lanes) in enumerate(tiles):
-            col_part[1, k, :, lanes] = jnp.sum(tree(jnp.add, totals[n]), axis=0, keepdims=True)
+    def sum_columns(pair, block):
+        tiles = tiles_of(pair)
+
+        def some(q, carry):
+            at = pl.ds(pl.multiple_of(q * LANES, LANES), LANES)
+            row_term = b_col[block, at, :]
+            out = []
+            for (k, lanes), total in zip(tiles, carry):
+                t = (prod[k, block, at, lanes] * row_term).reshape(4, 4, 8, LANES)
+                out.append(total + ((t[0] + t[1]) + (t[2] + t[3])))
+            return tuple(out)
+
+        start = (jnp.zeros((4, 8, LANES), jnp.float32),) * len(tiles)
+        totals = lax.fori_loop(0, chunks, some, start, unroll=2)
+        return [jnp.sum(tree(jnp.add, total), axis=0, keepdims=True) for total in totals]
+
+    def sum_first(pair):
+        for (k, lanes), part in zip(tiles_of(pair), sum_columns(pair, 0)):
+            col_part[1, k, :, lanes] = part
+
+    def sum_second(pair):
+        for (k, lanes), part in zip(tiles_of(pair), sum_columns(pair, 1)):
+            col_part[1, k, :, lanes] = col_part[1, k, :, lanes] + part
+
+    def all_chips(visit):
+        def one(n, carry):
+            visit((2 * n, 2 * n + 1))
+            return carry
+
+        lax.fori_loop(0, GROUP // 2, one, 0)
 
     def column_pass(iteration, visit):
         def start(message, k):
@@ -465,49 +523,72 @@
         pltpu.make_async_copy(view, view, col_recv.at[iteration]).wait()
         return col_in[iteration]
 
-    parts = column_pass(0, log_columns)
+    finish_log_rows(0)
+    all_chips(log_first)
+    finish_log_rows(1)
+    parts = column_pass(0, log_second)
     peak = jnp.max(parts, axis=0)
     total = jnp.sum(jnp.exp2(parts - peak[None]), axis=0)
     a = LOG2E * col_logw[...] - (peak + jnp.log2(total))
     a_all[slot] = a
     share_potential()
 
-    def spread(k, carry):
-        for i in range(2):
-            a_wide[i, k] = jnp.broadcast_to(a_all[k] + bias_of(i, k), (8, shard))
-        return carry
-
-    lax.fori_loop(0, GROUP, spread, 0)
-    step_rows = 32
-
-    def plan_rows(step, carry):
-        block = step // (rows // step_rows)
-        at = pl.ds(
-            pl.multiple_of(step % (rows // step_rows) * step_rows, step_rows), step_rows
-        )
-        totals = [jnp.zeros((step_rows // 8, 8, LANES), jnp.float32)] * 2
-        for k in range(GROUP):
-            t = jnp.exp2(
-                prod[k, block, at, :].reshape(step_rows // 8, 8, shard) + a_wide[block, k][None]
-            )
-            prod[k, block, at, :] = t.reshape(step_rows, shard)
-            totals[k % 2] = totals[k % 2] + sum(lane_tiles(t))
-        s_run[block, at, :] = sum(totals).reshape(step_rows, LANES)
-        return carry
-
-    lax.fori_loop(0, 2 * rows // step_rows, plan_rows, 0)
-    for i in range(2):
+    def spread_potential(pairs):
+        for p in pairs:
+            at = pair_at(p)
+            for k in (at, at + 1):
+                for i in range(2):
+                    a_wide[i, k] = jnp.broadcast_to(a_all[k] + bias_of(i, k), (8, shard))
+
+    step_rows = 128
+
+    def plan_rows(block, pairs, more):
+        slots = [pair_at(p) + c for p in pairs for c in range(2)]
+
+        def some(step, carry):
+            at = pl.ds(pl.multiple_of(step * step_rows, step_rows), step_rows)
+            totals = [jnp.zeros((step_rows // 8, 8, LANES), jnp.float32)] * 2
+            if more:
+                totals[0] = s_run[block, at, :].reshape(step_rows // 8, 8, LANES)
+            for n, k in enumerate(slots):
+                t = jnp.exp2(
+                    prod[k, block, at, :].reshape(step_rows // 8, 8, shard)
+                    + a_wide[block, k][None]
+                )
+                prod[k, block, at, :] = t.reshape(step_rows, shard)
+                totals[n % 2] = totals[n % 2] + sum(lane_tiles(t))
+            s_run[block, at, :] = sum(totals).reshape(step_rows, LANES)
+            return carry
+
+        lax.fori_loop(0, rows // step_rows, some, 0)
+
+    def fold_rows(block):
         for q in range(chunks):
             at = slice(q * LANES, (q + 1) * LANES)
-            row_part[1, row_slot, i, q : q + 1, :] = jnp.sum(
-                s_run[i, at, :].T, axis=0, keepdims=True
+            row_part[1, block, row_slot, q : q + 1, :] = jnp.sum(
+                s_run[block, at, :].T, axis=0, keepdims=True
             )
-    total = sum(exchange_rows(1))
-    scale = jnp.exp2(LOG2E * row_logw[...]) / total
-    spread_rows(scale)
-    b_keep[...] = b + LOG2E * row_logw[...] - jnp.log2(total)
-
-    total = jnp.sum(column_pass(1, sum_columns), axis=0)
+        send_row_sums(1, block)
+
+    def finish_rows(block):
+        total = sum(take_row_sums(1, block))
+        spread_rows(block, jnp.exp2(LOG2E * row_logw[block]) / total)
+        b_keep[block] = b_keep[block] + LOG2E * row_logw[block] - jnp.log2(total)
+
+    wait_potential(0)
+    spread_potential(range(4))
+    plan_rows(0, range(4), False)
+    wait_potential(1)
+    spread_potential(range(4, 8))
+    plan_rows(0, range(4, 8), True)
+    fold_rows(0)
+    plan_rows(1, range(8), False)
+    fold_rows(1)
+    finish_rows(0)
+    all_chips(sum_first)
+    finish_rows(1)
+
+    total = jnp.sum(column_pass(1, sum_second), axis=0)
     a = a + LOG2E * col_logw[...] - jnp.log2(total)
 
     row_out[...] = row_sq[...] / depth + dual_scale * b_keep[half]
@@ -520,8 +601,9 @@
     view = a_all.at[pl.ds(0, GROUP - 1)]
     pltpu.make_async_copy(view, view, a_send.at[0]).wait()
     for iteration in range(2):
-        view = row_part.at[iteration, pl.ds(0, len(row_peers))]
-        pltpu.make_async_copy(view, view, row_send.at[iteration]).wait()
+        for block in range(2):
+            view = row_part.at[iteration, block, pl.ds(0, len(row_peers))]
+            pltpu.make_async_copy(view, view, row_send.at[iteration, block]).wait()
         view = col_part.at[iteration, pl.ds(0, GROUP - 1)]
         pltpu.make_async_copy(view, view, col_send.at[iteration]).wait()
 
@@ -555,7 +637,7 @@
             pltpu.VMEM((GROUP, 1, shard), f32),
             pltpu.VMEM((2, GROUP, 8, shard), f32),
             pltpu.VMEM((rows // LANES, LANES), f32),
-            pltpu.VMEM((2, 2 * REPS, 2, rows // LANES, LANES), f32),
+            pltpu.VMEM((2, 2, 2 * REPS, rows // LANES, LANES), f32),
             pltpu.VMEM((2, GROUP, 1, shard), f32),
             pltpu.VMEM((2, GROUP, 1, shard), f32),
             pltpu.SemaphoreType.DMA((5,)),
@@ -565,9 +647,9 @@
             pltpu.SemaphoreType.DMA((1,)),
             pltpu.SemaphoreType.DMA((GROUP,)),
             pltpu.SemaphoreType.DMA((1,)),
-            pltpu.SemaphoreType.DMA((1,)),
             pltpu.SemaphoreType.DMA((2,)),
-            pltpu.SemaphoreType.DMA((2,)),
+            pltpu.SemaphoreType.DMA((2, 2)),
+            pltpu.SemaphoreType.DMA((2, 2)),
             pltpu.SemaphoreType.DMA((2,)),
             pltpu.SemaphoreType.DMA((2,)),
         ],

time: 72.5 us -> 64.6 us (0.89)
  Pallas kernels: 69.8 us -> 61.9 us
    pallas_call x1, Pallas kernels: 69.8 us -> 61.9 us  [per_device(): pl.pallas_call(kernel, out_shape=(jax.ShapeDtypeStruct((rows // LANES, LA...]
where the time goes in v4:
time: 64.6 us; the launch traced here: 64.4 us
  Pallas kernels  61.9 us (96%)
  local copies, waits for them, and re-layouts  1.87 us (3%)
  between operations  0.65 us (1%)
    pallas_call x1, Pallas kernels, per_device(): pl.pallas_call(kernel, out_shape=(jax.ShapeDtypeStruct((rows // LANES, LA...  61.9 us
    unnamed x6, local copies, waits for them, and re-layouts  1.87 us

profile of v4, /device:TPU:1, one launch (start us, length us, event | category | flops | bytes accessed | tf_op | source)
XLA Modules:
  0.0 64.4 jit_solution(5310134811398509651)
XLA Ops:
  0.6 61.9 %sinkhorn.1 = (f32[8,128]{1,0:T(8,128)}, f32[1,256]{1,0:T(1,128)}) custom-call(bf16[1024,256]{1,0:T(8,128)(2,1)} %source_hbm.1, bf16[256,256]{1,0:T(8,128)(2,1)} %target_hbm.1, f32[8,128]{1,0:T(8,128)} %bitcast.4, f32[1,256]{1,0:T(1,128)} %bitcast.6, s32[32,32]{1,0:T(8,128)} %support_hbm.1), custom_call_target="tpu_custom_call" | custom-call | tf_op jit(solution)/shard_map/sinkhorn/pallas_call | solution.py:616
  62.5 0.0 copy-start
  62.5 0.7 %copy-done = f32[8,128]{1,0:T(8,128)S(1)} copy-done((f32[8,128]{1,0:T(8,128)S(1)}, f32[8,128]{1,0:T(8,128)}, u32[]{:S(2)}) %copy-start) | copy-done | bytes 4120
  63.2 0.0 copy-start.1
  63.2 0.6 copy.9
  63.8 0.0 copy-done.1
  63.8 0.6 copy.10
Async XLA Ops:
  62.5 0.7 %copy-start = (f32[8,128]{1,0:T(8,128)S(1)}, f32[8,128]{1,0:T(8,128)}, u32[]{:S(2)}) copy-start(f32[8,128]{1,0:T(8,128)} %get-tuple-element.4) | copy-start | bytes 12292
  63.2 0.6 copy-start.1

commit v5 on v4

--- a/solution.py
+++ b/solution.py
@@ -45,6 +45,7 @@
     row_sq,
     row_part,
     col_part,
+    col_all,
     col_in,
     local_sem,
     logw_sem,
@@ -52,8 +53,8 @@
     src_recv,
     gather_send,
     gather_recv,
-    a_send,
-    a_recv,
+    all_send,
+    all_recv,
     row_send,
     row_recv,
     col_send,
@@ -148,16 +149,17 @@
         pl.semaphore_signal(barrier, inc=1, device_id=peer, device_id_type=MESH)
 
     loads[0].wait()
+    loads[4].wait()
     own = tgt[slot, :shard].astype(jnp.float32)
     own_sq = jnp.sum((own * own).T, axis=0, keepdims=True)
-    rest = -square_scale * own_sq
     parts = []
-    for _ in range(3):
-        parts.append(rest.astype(jnp.bfloat16))
-        rest = rest - parts[-1].astype(jnp.float32)
+    for rest in (-square_scale * own_sq, col_logw[...]):
+        for _ in range(3):
+            parts.append(rest.astype(jnp.bfloat16))
+            rest = rest - parts[-1].astype(jnp.float32)
     extra = tgt.shape[1] - shard
     tgt[slot, shard:] = jnp.concatenate(
-        parts + [jnp.zeros((extra - 3, depth), jnp.bfloat16)], axis=0
+        parts + [jnp.zeros((extra - 6, depth), jnp.bfloat16)], axis=0
     )
 
     pl.semaphore_wait(barrier, GROUP - 1 + len(row_peers))
@@ -208,7 +210,7 @@
     partner_slot = slot + 1 - 2 * core
     send_rows(0, 0)
     send_shard(slot, mine(1, 0))
-    for dz in (1, 3, 2):
+    for dz in (1, 3):
         send_shard(slot, mine(0, dz))
     send_shard(slot, partner_slot)
     logw_copy = pltpu.make_async_remote_copy(
@@ -221,33 +223,12 @@
     )
     logw_copy.start()
 
-    def share_potential():
-        def start(message, to):
-            step = message // 2
-            near = reached(step, 3) - reached(step, 4) + reached(step, 5)
-            pltpu.make_async_remote_copy(
-                src_ref=a_all.at[slot],
-                dst_ref=a_all.at[slot],
-                send_sem=a_send.at[0],
-                recv_sem=a_recv.at[1 - near],
-                device_id={"tile": base + to},
-                device_id_type=MESH,
-            ).start()
-
-        to_others(start)
-
-    near_messages = 7
-
-    def wait_potential(far):
-        view = a_all.at[pl.ds(0, GROUP - 1 - near_messages if far else near_messages)]
-        pltpu.make_async_copy(view, view, a_recv.at[far]).wait()
-
     def bias_of(i, k):
         tile = row_tiles[0] * (1 - i) + row_tiles[1] * i
         live = support[tile, rep * blocks + (base + k) // per_block]
         return (1.0 - live.astype(jnp.float32)) * NEG
 
-    for load in loads[1:]:
+    for load in loads[1:4]:
         load.wait()
 
     m_run[...] = jnp.full(m_run.shape, NEG, jnp.float32)
@@ -261,6 +242,7 @@
     view = src.at[0, pl.ds(0, quarter)]
     pltpu.make_async_copy(view, view, src_send.at[0]).wait()
     send_rows(2, 1)
+    send_shard(slot, mine(0, 2))
 
     def against(left, right):
         return lax.dot_general(
@@ -272,9 +254,9 @@
             for r in range(0, rows, 512):
                 stage[n, r : r + 512, :] = against(src[i, r : r + 512, :], tgt[k, :shard])
 
-    def column_term(i, k):
+    def column_term(k):
         parts = tgt[k, shard:].astype(jnp.float32)
-        return parts[0:1] + parts[1:2] + parts[2:3] + bias_of(i, k)
+        return parts[0:1] + parts[1:2] + parts[2:3]
 
     def update(i, pair, stage, terms):
         step = 32
@@ -317,11 +299,9 @@
         return half + other * (1 - 2 * half)
 
     def step_at(n):
-        late = reached(n, 4)
-        par = reached(n, 8) * (1 - half) + (late - reached(n, 12)) * half
-        p = n - 8 * reached(n, 8) * (1 - half) - 4 * (late + reached(n, 12)) * half
-        at = pair_at(p - reached(n, 16))
-        return half + par * (1 - 2 * half), (at, at + 1)
+        a, b, c = reached(n, 5), reached(n, 10), reached(n, 13)
+        at = pair_at(n - 5 * a - 3 * c)
+        return half * (1 - a) + (1 - half) * (a - b) + c, at
 
     row_slot = half * REPS + rep
 
@@ -357,58 +337,92 @@
             row_part[0, block, row_slot, q : q + 1, :] = peak + jnp.log2(total)
         send_row_sums(0, block)
 
-    turns = 8
+    def multiply(now, stage):
+        i, at = now
+        products(i, (at, at + 1), stage)
+
+    def fold_in(now, stage, terms):
+        i, at = now
+        update(i, (at, at + 1), stage, terms)
+
+    def terms_of(now):
+        i, at = now
+        bias = bias_of(i, at)
+        return [column_term(k) + bias for k in (at, at + 1)]
+
+    now = step_at(0)
     receive_theirs(0)
-    products(*step_at(0), stage_a)
+    multiply(now, stage_a)
+    fold_in(now, stage_a, terms_of(now))
+    receive(1)
+    wait_rows(0)
+    pass_rows(1)
+    pass_rows(3)
+    receive_theirs(1)
+    multiply(step_at(1), stage_a)
 
     def turn(j, carry):
         @pl.when(j == 6)
         def _():
             fold_log_rows(0)
 
-        now = step_at(2 * j)
+        now, later, last = carry
 
         @pl.when(j == 0)
         def _():
-            receive(1)
-            wait_rows(0)
-            pass_rows(1)
-            pass_rows(3)
             receive(2)
-            receive_theirs(1)
-
-        @pl.when(reached(j, 1) * (1 - reached(j, 4)) == 1)
-        def _():
-            @pl.when(j < 3)
-            def _():
-                receive(2 * j + 2)
-
-            receive_theirs(2 * j + 1)
-
-        later = step_at(2 * j + 1)
-        terms = [column_term(now[0], k) for k in now[1]]
-        products(*later, stage_b)
-        update(*now, stage_a, terms)
-
-        now = later
-
-        @pl.when(j < 3)
-        def _():
-            receive(2 * j + 3)
-            receive_theirs(2 * j + 2)
-
-        @pl.when(j == 3 - 2 * half)
+            receive(3)
+            receive_theirs(2)
+
+        @pl.when(j == 1)
+        def _():
+            receive(4)
+            receive_theirs(4)
+
+        @pl.when(j == 2)
+        def _():
+            receive(5)
+
+        @pl.when(j == 3)
+        def _():
+            receive(7)
+
+        @pl.when(j == 4)
+        def _():
+            receive_theirs(5)
+
+        @pl.when(j == 5)
+        def _():
+            receive_theirs(7)
+
+        terms = terms_of(now)
+        multiply(later, stage_b)
+        fold_in(now, stage_a, terms)
+
+        @pl.when(j == 0)
+        def _():
+            receive_theirs(3)
+
+        @pl.when(j == 1)
         def _():
             for i in (2, 1, 3):
                 wait_rows(i)
 
-        later = step_at(2 * j + 2)
-        terms = [column_term(now[0], k) for k in now[1]]
-        products(*later, stage_a)
-        update(*now, stage_b, terms)
-        return carry
-
-    lax.fori_loop(0, turns, turn, 0)
+        @pl.when(j == 2)
+        def _():
+            receive(6)
+
+        @pl.when(j == 4)
+        def _():
+            receive_theirs(6)
+
+        terms = terms_of(later)
+        multiply(last, stage_a)
+        fold_in(later, stage_b, terms)
+        return last, step_at(2 * j + 4), step_at(2 * j + 5)
+
+    now, _, _ = lax.fori_loop(0, 7, turn, (step_at(1), step_at(2), step_at(3)))
+    fold_in(now, stage_a, terms_of(now))
     fold_log_rows(1)
     logw_copy.wait()
 
@@ -499,13 +513,13 @@
 
         lax.fori_loop(0, GROUP // 2, one, 0)
 
-    def column_pass(iteration, visit):
+    def column_pass(visit):
         def start(message, k):
             pltpu.make_async_remote_copy(
-                src_ref=col_part.at[iteration, k],
-                dst_ref=col_in.at[iteration, message],
-                send_sem=col_send.at[iteration],
-                recv_sem=col_recv.at[iteration],
+                src_ref=col_part.at[1, k],
+                dst_ref=col_in.at[message],
+                send_sem=col_send.at[0],
+                recv_sem=col_recv.at[0],
                 device_id={"tile": base + k},
                 device_id_type=MESH,
             ).start()
@@ -518,32 +532,65 @@
         each_chip(both)
         visit((slot - core, slot - core + 1))
         start(GROUP - 2, partner_slot)
-        col_in[iteration, GROUP - 1] = col_part[iteration, slot]
-        view = col_in.at[iteration, pl.ds(0, GROUP - 1)]
-        pltpu.make_async_copy(view, view, col_recv.at[iteration]).wait()
-        return col_in[iteration]
+        col_in[GROUP - 1] = col_part[1, slot]
+        view = col_in.at[pl.ds(0, GROUP - 1)]
+        pltpu.make_async_copy(view, view, col_recv.at[0]).wait()
+        return col_in[...]
 
     finish_log_rows(0)
     all_chips(log_first)
     finish_log_rows(1)
-    parts = column_pass(0, log_second)
-    peak = jnp.max(parts, axis=0)
-    total = jnp.sum(jnp.exp2(parts - peak[None]), axis=0)
-    a = LOG2E * col_logw[...] - (peak + jnp.log2(total))
-    a_all[slot] = a
-    share_potential()
-
-    def spread_potential(pairs):
-        for p in pairs:
-            at = pair_at(p)
-            for k in (at, at + 1):
-                for i in range(2):
-                    a_wide[i, k] = jnp.broadcast_to(a_all[k] + bias_of(i, k), (8, shard))
+    groups_of_chips = ((0, 4), (4, 6), (6, 8))
+
+    def share_columns(g):
+        begin, end = groups_of_chips[g]
+        these = pl.ds(2 * begin, 2 * (end - begin))
+        col_all[slot, these] = col_part[0, these]
+
+        def start(message, to):
+            pltpu.make_async_remote_copy(
+                src_ref=col_part.at[0, these],
+                dst_ref=col_all.at[slot, these],
+                send_sem=all_send.at[g],
+                recv_sem=all_recv.at[g],
+                device_id={"tile": base + to},
+                device_id_type=MESH,
+            ).start()
+
+        to_others(start)
+
+    def wait_columns(g, sem):
+        begin, end = groups_of_chips[g]
+        view = col_all.at[pl.ds(0, GROUP - 1), pl.ds(2 * begin, 2 * (end - begin))]
+        pltpu.make_async_copy(view, view, sem).wait()
+
+    def take_columns(g):
+        wait_columns(g, all_recv.at[g])
+        begin, end = groups_of_chips[g]
+        for k in range(2 * begin, 2 * end):
+            parts = [col_all[i, k] for i in range(GROUP)]
+            peak = functools.reduce(jnp.maximum, parts)
+            total = sum(jnp.exp2(v - peak) for v in parts)
+            weights = tgt[k, shard:].astype(jnp.float32)
+            weights = weights[3:4] + weights[4:5] + weights[5:6]
+            a = LOG2E * weights - (peak + jnp.log2(total))
+            a_all[k] = a
+            for i in range(2):
+                a_wide[i, k] = jnp.broadcast_to(a + bias_of(i, k), (8, shard))
+
+    for g, (begin, end) in enumerate(groups_of_chips):
+
+        def one(n, carry):
+            log_second((2 * n, 2 * n + 1))
+            return carry
+
+        lax.fori_loop(begin, end, one, 0)
+        share_columns(g)
 
     step_rows = 128
 
-    def plan_rows(block, pairs, more):
-        slots = [pair_at(p) + c for p in pairs for c in range(2)]
+    def plan_rows(block, chips, more):
+        slots = range(2 * chips[0], 2 * chips[1])
 
         def some(step, carry):
             at = pl.ds(pl.multiple_of(step * step_rows, step_rows), step_rows)
@@ -575,21 +622,18 @@
         spread_rows(block, jnp.exp2(LOG2E * row_logw[block]) / total)
         b_keep[block] = b_keep[block] + LOG2E * row_logw[block] - jnp.log2(total)
 
-    wait_potential(0)
-    spread_potential(range(4))
-    plan_rows(0, range(4), False)
-    wait_potential(1)
-    spread_potential(range(4, 8))
-    plan_rows(0, range(4, 8), True)
+    for g, chips in enumerate(groups_of_chips):
+        take_columns(g)
+        plan_rows(0, chips, g > 0)
     fold_rows(0)
-    plan_rows(1, range(8), False)
+    plan_rows(1, (0, 8), False)
     fold_rows(1)
     finish_rows(0)
     all_chips(sum_first)
     finish_rows(1)
 
-    total = jnp.sum(column_pass(1, sum_second), axis=0)
-    a = a + LOG2E * col_logw[...] - jnp.log2(total)
+    total = jnp.sum(column_pass(sum_second), axis=0)
+    a = a_all[slot] + LOG2E * col_logw[...] - jnp.log2(total)
 
     row_out[...] = row_sq[...] / depth + dual_scale * b_keep[half]
     col_out[...] = own_sq / depth + dual_scale * a
@@ -598,14 +642,14 @@
     pltpu.make_async_copy(view, view, gather_send.at[0]).wait()
     view = src.at[0, pl.ds(0, 3 * quarter)]
     pltpu.make_async_copy(view, view, src_send.at[1]).wait()
-    view = a_all.at[pl.ds(0, GROUP - 1)]
-    pltpu.make_async_copy(view, view, a_send.at[0]).wait()
+    for g in range(len(groups_of_chips)):
+        wait_columns(g, all_send.at[g])
     for iteration in range(2):
         for block in range(2):
             view = row_part.at[iteration, block, pl.ds(0, len(row_peers))]
             pltpu.make_async_copy(view, view, row_send.at[iteration, block]).wait()
-        view = col_part.at[iteration, pl.ds(0, GROUP - 1)]
-        pltpu.make_async_copy(view, view, col_send.at[iteration]).wait()
+    view = col_in.at[pl.ds(0, GROUP - 1)]
+    pltpu.make_async_copy(view, view, col_send.at[0]).wait()
 
 
 def per_device(source, target, row_logw, col_logw, support):
@@ -639,19 +683,20 @@
             pltpu.VMEM((rows // LANES, LANES), f32),
             pltpu.VMEM((2, 2, 2 * REPS, rows // LANES, LANES), f32),
             pltpu.VMEM((2, GROUP, 1, shard), f32),
-            pltpu.VMEM((2, GROUP, 1, shard), f32),
+            pltpu.VMEM((GROUP, GROUP, 1, shard), f32),
+            pltpu.VMEM((GROUP, 1, shard), f32),
             pltpu.SemaphoreType.DMA((5,)),
             pltpu.SemaphoreType.DMA((2,)),
             pltpu.SemaphoreType.DMA((2,)),
             pltpu.SemaphoreType.DMA((REPS,)),
             pltpu.SemaphoreType.DMA((1,)),
             pltpu.SemaphoreType.DMA((GROUP,)),
-            pltpu.SemaphoreType.DMA((1,)),
-            pltpu.SemaphoreType.DMA((2,)),
+            pltpu.SemaphoreType.DMA((3,)),
+            pltpu.SemaphoreType.DMA((3,)),
             pltpu.SemaphoreType.DMA((2, 2)),
             pltpu.SemaphoreType.DMA((2, 2)),
-            pltpu.SemaphoreType.DMA((2,)),
-            pltpu.SemaphoreType.DMA((2,)),
+            pltpu.SemaphoreType.DMA((1,)),
+            pltpu.SemaphoreType.DMA((1,)),
         ],
         compiler_params=pltpu.CompilerParams(
             collective_id=0, has_side_effects=True, vmem_limit_bytes=63 * 1024 * 1024

time: 64.6 us -> 60.2 us (0.932)
  Pallas kernels: 61.9 us -> 57.5 us
    pallas_call x1, Pallas kernels: 61.9 us -> 57.5 us  [per_device(): pl.pallas_call(kernel, out_shape=(jax.ShapeDtypeStruct((rows // LANES, LA...]
where the time goes in v5:
time: 60.2 us; the launch traced here: 60.1 us
  Pallas kernels  57.5 us (96%)
  local copies, waits for them, and re-layouts  1.87 us (3%)
  between operations  0.65 us (1%)
    pallas_call x1, Pallas kernels, per_device(): pl.pallas_call(kernel, out_shape=(jax.ShapeDtypeStruct((rows // LANES, LA...  57.5 us
    unnamed x6, local copies, waits for them, and re-layouts  1.87 us

profile of v5, /device:TPU:1, one launch (start us, length us, event | category | flops | bytes accessed | tf_op | source)
XLA Modules:
  0.0 60.1 jit_solution(9663501410515297787)
XLA Ops:
  0.6 57.5 %sinkhorn.1 = (f32[8,128]{1,0:T(8,128)}, f32[1,256]{1,0:T(1,128)}) custom-call(bf16[1024,256]{1,0:T(8,128)(2,1)} %source_hbm.1, bf16[256,256]{1,0:T(8,128)(2,1)} %target_hbm.1, f32[8,128]{1,0:T(8,128)} %bitcast.4, f32[1,256]{1,0:T(1,128)} %bitcast.6, s32[32,32]{1,0:T(8,128)} %support_hbm.1), custom_call_target="tpu_custom_call" | custom-call | tf_op jit(solution)/shard_map/sinkhorn/pallas_call | solution.py:660
  58.2 0.0 copy-start
  58.2 0.7 %copy-done = f32[8,128]{1,0:T(8,128)S(1)} copy-done((f32[8,128]{1,0:T(8,128)S(1)}, f32[8,128]{1,0:T(8,128)}, u32[]{:S(2)}) %copy-start) | copy-done | bytes 4120
  58.9 0.0 copy-start.1
  58.9 0.6 copy.9
  59.5 0.0 copy-done.1
  59.5 0.6 copy.10
Async XLA Ops:
  58.2 0.7 %copy-start = (f32[8,128]{1,0:T(8,128)S(1)}, f32[8,128]{1,0:T(8,128)}, u32[]{:S(2)}) copy-start(f32[8,128]{1,0:T(8,128)} %get-tuple-element.4) | copy-start | bytes 12292
  58.9 0.6 %copy-start.1 = (f32[1,256]{1,0:T(1,128)S(1)}, f32[1,256]{1,0:T(1,128)}, u32[]{:S(2)}) copy-start(f32[1,256]{1,0:T(1,128)} %get-tuple-element.5) | copy-start | bytes 3076

commit v6 on v5

--- a/solution.py
+++ b/solution.py
@@ -280,6 +280,7 @@
     def receive(p):
         k = pair_at(p) + core
         wait_shard(k)
+        send_shard(k, partner_slot)
 
         @pl.when(core * 8 + p == 1)
         def _():
@@ -289,8 +290,6 @@
         @pl.when(core * reached(p, 2) * (1 - reached(p, 5)) == 1)
         def _():
             send_shard(k, mine(1, 0))
-
-        send_shard(k, partner_slot)
 
     def receive_theirs(p):
         wait_shard(pair_at(p) + 1 - core)
@@ -622,11 +621,15 @@
         spread_rows(block, jnp.exp2(LOG2E * row_logw[block]) / total)
         b_keep[block] = b_keep[block] + LOG2E * row_logw[block] - jnp.log2(total)
 
-    for g, chips in enumerate(groups_of_chips):
-        take_columns(g)
-        plan_rows(0, chips, g > 0)
+    take_columns(0)
+    plan_rows(0, (0, 4), False)
+    take_columns(1)
+    plan_rows(0, (4, 6), True)
+    plan_rows(1, (0, 4), False)
+    take_columns(2)
+    plan_rows(0, (6, 8), True)
     fold_rows(0)
-    plan_rows(1, (0, 8), False)
+    plan_rows(1, (4, 8), True)
     fold_rows(1)
     finish_rows(0)
     all_chips(sum_first)

time: 60.2 us -> 59.7 us (level)
  no operation moved by 1% of the time
where the time goes in v6:
time: 59.7 us; the launch traced here: 59.6 us
  Pallas kernels  57.1 us (96%)
  local copies, waits for them, and re-layouts  1.87 us (3%)
  between operations  0.65 us (1%)
    pallas_call x1, Pallas kernels, per_device(): pl.pallas_call(kernel, out_shape=(jax.ShapeDtypeStruct((rows // LANES, LA...  57.1 us
    unnamed x6, local copies, waits for them, and re-layouts  1.87 us

profile of v6, /device:TPU:1, one launch (start us, length us, event | category | flops | bytes accessed | tf_op | source)
XLA Modules:
  0.0 59.6 jit_solution(11263763433215712097)
XLA Ops:
  0.6 57.1 %sinkhorn.1 = (f32[8,128]{1,0:T(8,128)}, f32[1,256]{1,0:T(1,128)}) custom-call(bf16[1024,256]{1,0:T(8,128)(2,1)} %source_hbm.1, bf16[256,256]{1,0:T(8,128)(2,1)} %target_hbm.1, f32[8,128]{1,0:T(8,128)} %bitcast.4, f32[1,256]{1,0:T(1,128)} %bitcast.6, s32[32,32]{1,0:T(8,128)} %support_hbm.1), custom_call_target="tpu_custom_call" | custom-call | tf_op jit(solution)/shard_map/sinkhorn/pallas_call | solution.py:663
  57.7 0.0 copy-start
  57.7 0.7 %copy-done = f32[8,128]{1,0:T(8,128)S(1)} copy-done((f32[8,128]{1,0:T(8,128)S(1)}, f32[8,128]{1,0:T(8,128)}, u32[]{:S(2)}) %copy-start) | copy-done | bytes 4120
  58.4 0.0 copy-start.1
  58.4 0.6 copy.9
  59.0 0.0 copy-done.1
  59.0 0.6 copy.10
Async XLA Ops:
  57.7 0.7 %copy-start = (f32[8,128]{1,0:T(8,128)S(1)}, f32[8,128]{1,0:T(8,128)}, u32[]{:S(2)}) copy-start(f32[8,128]{1,0:T(8,128)} %get-tuple-element.4) | copy-start | bytes 12292
  58.4 0.6 %copy-start.1 = (f32[1,256]{1,0:T(1,128)S(1)}, f32[1,256]{1,0:T(1,128)}, u32[]{:S(2)}) copy-start(f32[1,256]{1,0:T(1,128)} %get-tuple-element.5) | copy-start | bytes 3076

commit v7 on v6

--- a/solution.py
+++ b/solution.py
@@ -494,7 +494,7 @@
             return tuple(out)
 
         start = (jnp.zeros((4, 8, LANES), jnp.float32),) * len(tiles)
-        totals = lax.fori_loop(0, chunks, some, start, unroll=2)
+        totals = lax.fori_loop(0, chunks, some, start, unroll=4)
         return [jnp.sum(tree(jnp.add, total), axis=0, keepdims=True) for total in totals]
 
     def sum_first(pair):
@@ -633,13 +633,6 @@
     fold_rows(1)
     finish_rows(0)
     all_chips(sum_first)
-    finish_rows(1)
-
-    total = jnp.sum(column_pass(sum_second), axis=0)
-    a = a_all[slot] + LOG2E * col_logw[...] - jnp.log2(total)
-
-    row_out[...] = row_sq[...] / depth + dual_scale * b_keep[half]
-    col_out[...] = own_sq / depth + dual_scale * a
 
     view = tgt.at[pl.ds(0, GROUP - 1)]
     pltpu.make_async_copy(view, view, gather_send.at[0]).wait()
@@ -647,6 +640,15 @@
     pltpu.make_async_copy(view, view, src_send.at[1]).wait()
     for g in range(len(groups_of_chips)):
         wait_columns(g, all_send.at[g])
+
+    finish_rows(1)
+
+    total = jnp.sum(column_pass(sum_second), axis=0)
+    a = a_all[slot] + LOG2E * col_logw[...] - jnp.log2(total)
+
+    row_out[...] = row_sq[...] / depth + dual_scale * b_keep[half]
+    col_out[...] = own_sq / depth + dual_scale * a
+
     for iteration in range(2):
         for block in range(2):
             view = row_part.at[iteration, block, pl.ds(0, len(row_peers))]

time: 59.7 us -> 59.5 us (level)
  no operation moved by 1% of the time
where the time goes in v7:
time: 59.5 us; the launch traced here: 59.3 us
  Pallas kernels  56.8 us (95%)
  local copies, waits for them, and re-layouts  1.87 us (3%)
  between operations  0.65 us (1%)
    pallas_call x1, Pallas kernels, per_device(): pl.pallas_call(kernel, out_shape=(jax.ShapeDtypeStruct((rows // LANES, LA...  56.8 us
    unnamed x6, local copies, waits for them, and re-layouts  1.87 us

profile of v7, /device:TPU:1, one launch (start us, length us, event | category | flops | bytes accessed | tf_op | source)
XLA Modules:
  0.0 59.3 jit_solution(8490320075489074838)
XLA Ops:
  0.6 56.8 %sinkhorn.1 = (f32[8,128]{1,0:T(8,128)}, f32[1,256]{1,0:T(1,128)}) custom-call(bf16[1024,256]{1,0:T(8,128)(2,1)} %source_hbm.1, bf16[256,256]{1,0:T(8,128)(2,1)} %target_hbm.1, f32[8,128]{1,0:T(8,128)} %bitcast.4, f32[1,256]{1,0:T(1,128)} %bitcast.6, s32[32,32]{1,0:T(8,128)} %support_hbm.1), custom_call_target="tpu_custom_call" | custom-call | tf_op jit(solution)/shard_map/sinkhorn/pallas_call | solution.py:665
  57.5 0.0 copy-start
  57.5 0.7 %copy-done = f32[8,128]{1,0:T(8,128)S(1)} copy-done((f32[8,128]{1,0:T(8,128)S(1)}, f32[8,128]{1,0:T(8,128)}, u32[]{:S(2)}) %copy-start) | copy-done | bytes 4120
  58.1 0.0 copy-start.1
  58.1 0.6 copy.9
  58.7 0.0 copy-done.1
  58.8 0.6 copy.10
Async XLA Ops:
  57.5 0.7 %copy-start = (f32[8,128]{1,0:T(8,128)S(1)}, f32[8,128]{1,0:T(8,128)}, u32[]{:S(2)}) copy-start(f32[8,128]{1,0:T(8,128)} %get-tuple-element.4) | copy-start | bytes 12292
  58.1 0.6 %copy-start.1 = (f32[1,256]{1,0:T(1,128)S(1)}, f32[1,256]{1,0:T(1,128)}, u32[]{:S(2)}) copy-start(f32[1,256]{1,0:T(1,128)} %get-tuple-element.5) | copy-start | bytes 3076

commit v8 on v7

--- a/solution.py
+++ b/solution.py
@@ -586,7 +586,7 @@
         lax.fori_loop(begin, end, one, 0)
         share_columns(g)
 
-    step_rows = 128
+    step_rows = 256
 
     def plan_rows(block, chips, more):
         slots = range(2 * chips[0], 2 * chips[1])

time: 59.5 us -> 60.2 us (1.012)
  Pallas kernels: 56.8 us -> 57.5 us
    pallas_call x1, Pallas kernels: 56.8 us -> 57.5 us  [per_device(): pl.pallas_call(kernel, out_shape=(jax.ShapeDtypeStruct((rows // LANES, LA...]
where the time goes in v8:
time: 60.2 us; the launch traced here: 60 us
  Pallas kernels  57.5 us (96%)
  local copies, waits for them, and re-layouts  1.87 us (3%)
  between operations  0.65 us (1%)
    pallas_call x1, Pallas kernels, per_device(): pl.pallas_call(kernel, out_shape=(jax.ShapeDtypeStruct((rows // LANES, LA...  57.5 us
    unnamed x6, local copies, waits for them, and re-layouts  1.87 us

profile of v8, /device:TPU:1, one launch (start us, length us, event | category | flops | bytes accessed | tf_op | source)
XLA Modules:
  0.0 60.0 jit_solution(9232694815845300431)
XLA Ops:
  0.6 57.5 %sinkhorn.1 = (f32[8,128]{1,0:T(8,128)}, f32[1,256]{1,0:T(1,128)}) custom-call(bf16[1024,256]{1,0:T(8,128)(2,1)} %source_hbm.1, bf16[256,256]{1,0:T(8,128)(2,1)} %target_hbm.1, f32[8,128]{1,0:T(8,128)} %bitcast.4, f32[1,256]{1,0:T(1,128)} %bitcast.6, s32[32,32]{1,0:T(8,128)} %support_hbm.1), custom_call_target="tpu_custom_call" | custom-call | tf_op jit(solution)/shard_map/sinkhorn/pallas_call | solution.py:665
  58.1 0.0 copy-start
  58.1 0.7 %copy-done = f32[8,128]{1,0:T(8,128)S(1)} copy-done((f32[8,128]{1,0:T(8,128)S(1)}, f32[8,128]{1,0:T(8,128)}, u32[]{:S(2)}) %copy-start) | copy-done | bytes 4120
  58.8 0.0 copy-start.1
  58.8 0.6 copy.9
  59.4 0.0 copy-done.1
  59.4 0.6 copy.10
Async XLA Ops:
  58.1 0.7 %copy-start = (f32[8,128]{1,0:T(8,128)S(1)}, f32[8,128]{1,0:T(8,128)}, u32[]{:S(2)}) copy-start(f32[8,128]{1,0:T(8,128)} %get-tuple-element.4) | copy-start | bytes 12292
  58.8 0.6 %copy-start.1 = (f32[1,256]{1,0:T(1,128)S(1)}, f32[1,256]{1,0:T(1,128)}, u32[]{:S(2)}) copy-start(f32[1,256]{1,0:T(1,128)} %get-tuple-element.5) | copy-start | bytes 3076
